TPU v7x, 32 devices: a whole 2x2x4 slice. The times are simulated.
32 devices in a mesh: grp: 2 (over y), ep: 4 (over x, core), sub: 4 (over z).
Axes of the slice: x: 2, y: 2, z: 4, core: 2. Of those that a mesh axis runs over, the one named last changes fastest.
Arguments:
- tokens: bfloat16 [2, 512, 2880], P(None, ('grp', 'ep', 'sub')), parts along dimension 1
- norm_gain: float32 [2880], replicated, may hold values from 0.25 to 1.75
- copy_ids: int32 [2, 512, 4], P(None, ('grp', 'ep', 'sub')), parts along dimension 1, may hold values from 0 to 7, as said below
- gate_scores: float32 [2, 512, 4], P(None, ('grp', 'ep', 'sub')), parts along dimension 1, may hold values from 0.05 to 1
- inner_codes: bfloat16 [8, 2880, 2, 2880], P('ep', None, None, 'sub'), may hold values from -6 to 6
- inner_scales: bfloat16 [8, 90, 2, 2880], P('ep', None, None, 'sub'), may hold values from 0.0099487305 to 0.029907227
- down_codes: bfloat16 [8, 2880, 2880], P('ep', None, 'sub'), may hold values from -6 to 6
- down_scales: bfloat16 [8, 90, 2880], P('ep', None, 'sub'), may hold values from 0.014953613 to 0.044921875
Outputs:
- moe_out: bfloat16 [2, 512, 2880], P(None, ('grp', 'ep', 'sub')), parts along dimension 1
There are 2 independent parts, one for each index of `grp`. A program takes and returns all parts, laid end to end along the dimension named above; an argument that names none is the same for every part. Nothing has to cross between parts.
Inputs may be any that keep to these rules, and one draw needn't show every extreme that they name: `copy_ids`: each token names 4 different experts. Among the tokens of one device in one step (aligned blocks of 16 tokens) no expert is named more than 12 times, and in each step one expert is named exactly 12 times by the tokens of every device.
All inputs are finite; a program needn't handle non-finite values.
Results may differ from a plain program's by a relative error of at most 0.0085.
Values may be sent and summed in bfloat16 or wider, within the bound.
No kernel may reach another device: no remote copies, remote signals or barrier semaphores. Data moves between devices by JAX's collectives and lax.ppermute only.
A program may use at most 192 MiB of HBM per device.

v0:
```python
import functools

import jax
import jax.numpy as jnp
from jax import lax
from jax.experimental import pallas as pl
from jax.experimental.pallas import tpu as pltpu
from jax.sharding import PartitionSpec as P

epsilon = 1e-05
swish_beta = 1.702
META = 64
LANES = 128
VMEM_LIMIT = 24 * 1024 * 1024
HINT = pl.CostEstimate(flops=1024, bytes_accessed=1024, transcendentals=0)
F32 = jnp.float32
BF16 = jnp.bfloat16


def params():
    return pltpu.CompilerParams(vmem_limit_bytes=VMEM_LIMIT)


def in_hbm(x):
    return pltpu.with_memory_space_constraint(x, pltpu.HBM)


def dot(a, b, contract):
    return lax.dot_general(a, b, (contract, ((), ())), preferred_element_type=F32)


def pack_kernel(tokens_ref, gain_ref, ids_ref, scores_ref, out_ref):
    steps, rows, width = tokens_ref.shape
    top = ids_ref.shape[1]
    gain = gain_ref[...].reshape(1, width)
    eye = (
        lax.broadcasted_iota(jnp.int32, (rows, rows), 0)
        == lax.broadcasted_iota(jnp.int32, (rows, rows), 1)
    ).astype(F32)

    def column(row):
        return jnp.sum(eye * row, axis=1, keepdims=True)

    for s in range(steps):
        values = tokens_ref[s].astype(F32)
        mean = jnp.mean(values * values, axis=-1, keepdims=True)
        normed = (values * lax.rsqrt(mean + epsilon) * gain).astype(BF16)
        at = slice(s * rows, (s + 1) * rows)
        out_ref[at, :width] = normed
        scores = scores_ref[s]
        weights = scores / jnp.sum(scores, axis=0, keepdims=True)
        high = weights.astype(BF16)
        rest = weights - high.astype(F32)
        middle = rest.astype(BF16)
        low = (rest - middle.astype(F32)).astype(BF16)
        lane = lax.broadcasted_iota(jnp.int32, (rows, META), 1)
        meta = jnp.zeros((rows, META), F32)
        parts = (ids_ref[s].astype(F32), high.astype(F32), middle.astype(F32), low.astype(F32))
        for p, part in enumerate(parts):
            for k in range(top):
                meta = jnp.where(lane == p * top + k, column(part[k : k + 1]), meta)
        out_ref[at, width:] = meta.astype(BF16)


def pack(tokens, gain, ids, scores):
    steps, rows, width = tokens.shape
    return pl.pallas_call(
        pack_kernel,
        out_shape=jax.ShapeDtypeStruct((steps * rows, width + META), BF16),
        compiler_params=params(),
    )(
        in_hbm(tokens),
        in_hbm(gain),
        in_hbm(jnp.transpose(ids, (0, 2, 1))),
        in_hbm(jnp.transpose(scores, (0, 2, 1))),
    )


def dequant_kernel(codes_ref, scales_ref, _after_ref, out_ref, mark_ref):
    width = codes_ref.shape[2]
    scales = scales_ref[0]
    blocks = scales.shape[1]
    chunk = 256 if len(out_ref.shape) == 3 else out_ref.shape[3]
    for at in range(0, width, chunk):
        end = min(at + chunk, width)
        column = lax.broadcasted_iota(jnp.int32, (blocks, end - at), 1) + at
        block = lax.broadcasted_iota(jnp.int32, (blocks, end - at), 0)
        first = block * (width // blocks)
        inside = jnp.logical_and(column >= first, column < first + width // blocks)
        wide = dot(scales, inside.astype(F32).astype(BF16), ((1,), (0,)))
        value = (codes_ref[0, :, at:end].astype(F32) * wide).astype(BF16)
        if len(out_ref.shape) == 3:
            out_ref[0, :, at:end] = value
        else:
            out_ref[0, at // chunk] = value
    mark_ref[...] = jnp.zeros_like(mark_ref)


def dequant(codes, scales, after, pieces=1):
    count, rows, width = codes.shape
    blocks = scales.shape[2]
    shape = (count, rows, width) if pieces == 1 else (count, pieces, rows, width // pieces)
    return pl.pallas_call(
        dequant_kernel,
        grid=(count,),
        in_specs=[
            pl.BlockSpec((1, rows, width), lambda i: (i, 0, 0)),
            pl.BlockSpec((1, rows, blocks), lambda i: (i, 0, 0)),
            pl.BlockSpec(memory_space=pl.ANY),
        ],
        out_specs=[
            pl.BlockSpec((1,) + shape[1:], lambda i: (i,) + (0,) * (len(shape) - 1)),
            pl.BlockSpec((8, LANES), lambda i: (0, 0)),
        ],
        out_shape=[
            jax.ShapeDtypeStruct(shape, BF16),
            jax.ShapeDtypeStruct((8, LANES), F32),
        ],
        compiler_params=params(),
        cost_estimate=HINT,
    )(in_hbm(codes), scales, after)


def join_kernel(count, pieces, *refs):
    outs = refs[-pieces:]
    rows, size = refs[0].shape[0], outs[0].shape[0]
    for p, out_ref in enumerate(outs):
        if size >= rows:
            for k in range(size // rows):
                out_ref[k * rows : (k + 1) * rows] = refs[p * (size // rows) + k][...]
        else:
            at = p * size % rows
            out_ref[...] = refs[p * size // rows][at : at + size]


def join(parts, after, pieces=1):
    rows, width = parts[0].shape
    count = len(parts)
    size = count * rows // pieces
    return pl.pallas_call(
        functools.partial(join_kernel, count, pieces),
        grid=(1,),
        in_specs=[pl.BlockSpec((rows, width), lambda i: (0, 0))] * count
        + [pl.BlockSpec(memory_space=pl.ANY)] * len(after),
        out_specs=[pl.BlockSpec((size, width), lambda i: (0, 0))] * pieces,
        out_shape=[jax.ShapeDtypeStruct((size, width), BF16)] * pieces,
        compiler_params=params(),
        cost_estimate=HINT,
    )(*parts, *after)


class Plan:
    def __init__(self, first, rows, holds, slots, subs, group, top, eps):
        self.first, self.rows = first, rows
        self.holds = holds
        self.slots, self.subs, self.group, self.top, self.eps = slots, subs, group, top, eps

    def part(self, begin, rows):
        return Plan(
            self.first + begin, rows, self.holds, self.slots, self.subs, self.group, self.top, self.eps
        )


def chosen(meta, expert, top):
    named = jnp.zeros((meta.shape[0], 1), F32)
    weight = jnp.zeros((meta.shape[0], 1), F32)
    for k in range(top):
        at = meta.shape[1] - META + k
        hit = (meta[:, at : at + 1] == expert).astype(F32)
        total = (
            meta[:, at + top : at + top + 1]
            + meta[:, at + 2 * top : at + 2 * top + 1]
            + meta[:, at + 3 * top : at + 3 * top + 1]
        )
        named = named + hit
        weight = weight + hit * total
    return named, weight


def order_mask(count, plan, sub):
    def key(dim):
        t = lax.broadcasted_iota(jnp.int32, (count, count), dim)
        block = lax.rem(lax.div(t, plan.group), plan.subs)
        return t + (jnp.bitwise_xor(block, sub) - block) * plan.group

    return (key(1) < key(0)).astype(BF16)


def route(metas, plan, ep, sub):
    count = metas[0].shape[0]
    earlier = order_mask(count, plan, sub)
    lane = lax.broadcasted_iota(jnp.int32, (count, LANES), 1)
    start = jnp.zeros((1, 1), F32)
    result = []
    bounds = []
    for column, meta in enumerate(metas):
        if column:
            start = jnp.maximum(start, float(plan.holds[column - 1]))
        found = []
        flags = jnp.zeros((count, LANES), F32)
        for slot in range(plan.slots):
            named, weight = chosen(meta, (ep * plan.slots + slot).astype(F32), plan.top)
            found.append((named, weight))
            flags = jnp.where(lane == slot, named, flags)
        prefix = dot(earlier, flags.astype(BF16), ((1,), (0,)))
        places = []
        for slot, (named, weight) in enumerate(found):
            place = jnp.where(named > 0.0, prefix[:, slot : slot + 1] + start, -1.0)
            places.append((place, weight))
            end = start + jnp.sum(named, axis=0, keepdims=True)
            bounds.append((slot, start, end))
            start = end
        result.append(places)
    return result, bounds


def slot_masks(bounds, plan):
    row = lax.broadcasted_iota(jnp.int32, (1, plan.rows), 1).astype(F32) + float(plan.first)
    masks = []
    for slot in range(plan.slots):
        mask = jnp.zeros((1, plan.rows), F32)
        for which, start, end in bounds:
            if which == slot:
                mask = mask + jnp.logical_and(row >= start, row < end).astype(F32)
        masks.append(mask)
    return masks


def rows_of(places, plan):
    return (
        lax.broadcasted_iota(jnp.int32, (places.shape[0], plan.rows), 1).astype(F32)
        + float(plan.first)
        == places
    )


def metas_of(layout, refs, width):
    metas, at = [], 0
    for count in layout:
        several = [ref[:, width:].astype(F32) for ref in refs[at : at + count]]
        metas.append(jnp.concatenate(several, axis=0))
        at += count
    return metas


def rows_kernel(plan, layout, place_ref, *refs):
    arrays = sum(layout)
    tokens = refs[:arrays]
    most_ref = refs[arrays]
    outs = refs[arrays + 1 :]
    width = outs[0].shape[0]
    ep, sub = place_ref[0], place_ref[1]
    metas = metas_of(layout, tokens, width)
    columns, bounds = route(metas, plan, ep, sub)
    begin = 0
    masks = slot_masks(bounds, plan)
    for _rows, mask_ref, high_ref, low_ref in zip(*[iter(outs)] * 4):
        size = mask_ref.shape[1]
        part = plan.part(begin, size)
        mask_ref[...] = jnp.zeros_like(mask_ref)
        for slot, mask in enumerate(masks):
            mask_ref[slot : slot + 1] = mask[:, begin : begin + size]
        at = 0
        for places in columns:
            mix = None
            for place, weight in places:
                term = jnp.where(rows_of(place, part), weight, 0.0)
                mix = term if mix is None else mix + term
            high = mix.astype(BF16)
            here = slice(at, at + mix.shape[0])
            high_ref[here] = high
            low_ref[here] = (mix - high.astype(F32)).astype(BF16)
            at += mix.shape[0]
        begin += size
    hots = []
    for places in columns:
        hot = None
        for place, _weight in places:
            hit = rows_of(place, plan).astype(F32)
            hot = hit if hot is None else hot + hit
        hots.append(hot.astype(BF16))
    hot = jnp.concatenate(hots, axis=0) if len(hots) > 1 else hots[0]
    chunk = 256
    for at in range(0, width, chunk):
        end = min(at + chunk, width)
        several = [ref[:, at:end] for ref in tokens]
        total = dot(jnp.concatenate(several, axis=0), hot, ((0,), (0,)))
        begin = 0
        for rows_ref in outs[::4]:
            rows_ref[at:end] = total[:, begin : begin + rows_ref.shape[1]].astype(BF16)
            begin += rows_ref.shape[1]
    lane = lax.broadcasted_iota(jnp.int32, (metas[0].shape[0], LANES), 1).astype(F32)
    owner = lax.div(lax.broadcasted_iota(jnp.int32, (1, LANES), 1), plan.slots)
    start = [jnp.zeros((1, 1), F32)] * plan.eps
    for column, meta in enumerate(metas):
        flags = jnp.zeros((meta.shape[0], LANES), F32)
        for k in range(plan.top):
            flags = flags + (meta[:, k : k + 1] == lane).astype(F32)
        counts = jnp.sum(flags, axis=0, keepdims=True)
        for e in range(plan.eps):
            if column:
                start[e] = jnp.maximum(start[e], float(plan.holds[column - 1]))
            start[e] = start[e] + jnp.sum(
                jnp.where(owner == e, counts, 0.0), axis=1, keepdims=True
            )
    most_ref[...] = jnp.broadcast_to(functools.reduce(jnp.maximum, start), most_ref.shape)


def rows_in(plan, place, held, split=None):
    layout = tuple(len(arrays) for arrays in held)
    tokens = [t for arrays in held for t in arrays]
    width = tokens[0].shape[1] - META
    total = sum(t.shape[0] for t in tokens)
    split = split or (plan.rows,)
    shapes = [jax.ShapeDtypeStruct((8, LANES), F32)]
    for size in split:
        shapes.append(jax.ShapeDtypeStruct((width, size), BF16))
        shapes.append(jax.ShapeDtypeStruct((8, size), F32))
        shapes.append(jax.ShapeDtypeStruct((total, size), BF16))
        shapes.append(jax.ShapeDtypeStruct((total, size), BF16))
    specs = [pl.BlockSpec(shape.shape, lambda i: (0, 0)) for shape in shapes]
    return pl.pallas_call(
        functools.partial(rows_kernel, plan, layout),
        grid=(1,),
        in_specs=[pl.BlockSpec(memory_space=pltpu.SMEM)]
        + [pl.BlockSpec(t.shape, lambda i: (0, 0)) for t in tokens],
        out_specs=specs,
        out_shape=shapes,
        compiler_params=params(),
        cost_estimate=HINT,
    )(place, *tokens)


def inner_kernel(plan, rows_ref, mask_ref, weight_ref, *refs):
    act_ref, mark_ref = refs[-2:]
    gating = upward = None
    for slot in range(plan.slots):
        gate = dot(weight_ref[slot, 0], rows_ref[...], ((1,), (0,)))
        up = dot(weight_ref[slot, 1], rows_ref[...], ((1,), (0,)))
        if slot == 0:
            gating, upward = gate, up
        else:
            mine = mask_ref[slot : slot + 1] > 0.0
            gating = jnp.where(mine, gate, gating)
            upward = jnp.where(mine, up, upward)
    act_ref[...] = (gating * jax.nn.sigmoid(swish_beta * gating) * (upward + 1.0)).astype(BF16)
    mark_ref[...] = jnp.zeros_like(mark_ref)


def piece(total):
    for size in (240, 120, 72, 40, 24, 16, 8):
        if total % size == 0:
            return size
    return total


def inner(plan, rows, mask, weights, after):
    slots, _two, units, width = weights.shape
    block = piece(units)
    return pl.pallas_call(
        functools.partial(inner_kernel, plan),
        grid=(units // block,),
        in_specs=[
            pl.BlockSpec(rows.shape, lambda i: (0, 0)),
            pl.BlockSpec(mask.shape, lambda i: (0, 0)),
            pl.BlockSpec((slots, 2, block, width), lambda i: (0, 0, i, 0)),
        ]
        + [pl.BlockSpec(memory_space=pl.ANY)] * len(after),
        out_specs=[
            pl.BlockSpec((block, rows.shape[1]), lambda i: (i, 0)),
            pl.BlockSpec((8, LANES), lambda i: (0, 0)),
        ],
        out_shape=[
            jax.ShapeDtypeStruct((units, rows.shape[1]), BF16),
            jax.ShapeDtypeStruct((8, LANES), F32),
        ],
        compiler_params=params(),
        cost_estimate=HINT,
    )(rows, mask, weights, *after)


def add_blocks(plan, which, ends, sub, parts, weight_ref):
    total = None
    for at, k in enumerate(which):
        x = parts[at][...]
        if k == 3 and ends:
            inside = jnp.logical_or(sub == 1, sub == 2)
            x = jnp.where(inside, x, parts[at + 1][...])
        weights = weight_ref[0, 0 if len(which) == 1 else jnp.bitwise_xor(sub, k)]
        term = dot(weights, x, ((1,), (0,)))
        total = term if total is None else total + term
    return total


def pick(slot, plan, mask_ref, new, old_ref, here):
    @pl.when(slot == 0)
    def _():
        old_ref[here] = new.astype(old_ref.dtype)

    @pl.when(slot > 0)
    def _():
        mine = mask_ref[0:1]
        for s in range(1, plan.slots):
            mine = jnp.where(slot == s, mask_ref[s : s + 1], mine)
        old_ref[here] = jnp.where(mine > 0.0, new.astype(old_ref.dtype), old_ref[here])


def part_kernel(plan, which, place_ref, mask_ref, *refs):
    count = len(which)
    parts, weight_ref, out_ref = refs[:count], refs[count], refs[-1]
    slot, chunk = pl.program_id(0), pl.program_id(1)
    size = weight_ref.shape[2]
    here = pl.ds(pl.multiple_of(chunk * size, size), size)
    out = add_blocks(plan, which, False, place_ref[1], parts, weight_ref)
    pick(slot, plan, mask_ref, out, out_ref, here)


def outer_kernel(plan, which, ends, first, before, place_ref, mask_ref, high_ref, low_ref, *refs):
    count = len(which) + ends
    parts = refs[:count]
    first_ref = refs[count] if first else None
    befores = refs[count + first : count + first + before]
    weight_ref = refs[count + first + before]
    keep_ref, send_ref, sum_ref = refs[-3:]
    slot, chunk = pl.program_id(0), pl.program_id(1)
    size = weight_ref.shape[2]
    here = pl.ds(pl.multiple_of(chunk * size, size), size)
    out = add_blocks(plan, which, ends, place_ref[1], parts, weight_ref)
    if first:
        out = out + first_ref[here]
    pick(slot, plan, mask_ref, out, sum_ref, here)

    @pl.when(jnp.logical_and(slot == plan.slots - 1, chunk == pl.num_programs(1) - 1))
    def _():
        done = sum_ref[...]
        half = keep_ref.shape[1]
        for c in range(keep_ref.shape[0]):
            for h, ref in enumerate((keep_ref, send_ref)):
                if 2 * c * half >= high_ref.shape[0]:
                    ref[c] = jnp.zeros((half, ref.shape[2]), BF16)
                    continue
                at = slice((2 * c + h) * half, (2 * c + h + 1) * half)
                value = dot(high_ref[at], done, ((1,), (1,))) + dot(low_ref[at], done, ((1,), (1,)))
                if before and c < befores[h].shape[0]:
                    value = value + befores[h][c].astype(F32)
                ref[c] = value.astype(BF16)


def outer_call(kernel, place, operands, weights, which, after, shapes, scratch):
    slots, subs, columns_out, units = weights.shape
    size = 240 if columns_out % 240 == 0 else columns_out

    def whole(x):
        return pl.BlockSpec(x.shape, lambda i, j, p: (0,) * len(x.shape))

    if len(which) == 1:
        weight_spec = pl.BlockSpec(
            (1, 1, size, units), lambda i, j, p: (i, jnp.bitwise_xor(p[1], which[0]), j, 0)
        )
    else:
        weight_spec = pl.BlockSpec((1, subs, size, units), lambda i, j, p: (i, 0, j, 0))
    return pl.pallas_call(
        kernel,
        grid_spec=pltpu.PrefetchScalarGridSpec(
            num_scalar_prefetch=1,
            grid=(slots, columns_out // size),
            in_specs=[whole(x) for x in operands]
            + [weight_spec]
            + [pl.BlockSpec(memory_space=pl.ANY)] * len(after),
            out_specs=[whole(x) for x in shapes],
            scratch_shapes=scratch,
        ),
        out_shape=shapes,
        compiler_params=params(),
        cost_estimate=HINT,
    )(place, *operands, in_hbm(weights), *after)


def outer_part(plan, place, mask, parts, weights, after):
    which = tuple(range(len(parts)))
    shape = jax.ShapeDtypeStruct((weights.shape[2], parts[0].shape[1]), F32)
    kernel = functools.partial(part_kernel, plan, which)
    return outer_call(kernel, place, [mask, *parts], weights, which, after, [shape], [])[0]


def outer(plan, place, mixed, parts, befores, weights, columns, first=None):
    subs, columns_out = weights.shape[1:3]
    rows = parts[0].shape[1]
    half = plan.group * plan.subs
    which = tuple(range(subs)) if first is None else (subs - 1,)
    ends = len(parts) > len(which)
    firsts = [] if first is None else [first]
    result = jax.ShapeDtypeStruct((columns, half, columns_out), BF16)
    return outer_call(
        functools.partial(outer_kernel, plan, which, ends, len(firsts), len(befores)),
        place,
        [mixed[0], in_hbm(mixed[1]), in_hbm(mixed[2]), *parts, *firsts, *befores],
        weights,
        which,
        (),
        [result, result],
        [pltpu.VMEM((columns_out, rows), BF16)],
    )


def finish_kernel(subs, columns, place_ref, *refs):
    out_ref = refs[-1]
    sub = place_ref[1]
    width = refs[0].shape[1]
    steps, rows, _ = out_ref.shape
    sums = []
    for k in range(subs):
        value = refs[k * columns][...].astype(F32)
        for j in range(1, columns):
            value = value + refs[k * columns + j][...].astype(F32)
        sums.append(value)
    for b in range(subs):
        value = sums[0]
        for k in range(1, subs):
            value = jnp.where(jnp.bitwise_xor(sub, k) == b, sums[k], value)
        value = value.astype(BF16)
        for s in range(steps):
            out_ref[s, :, b * width : (b + 1) * width] = value[s * rows : (s + 1) * rows]


def finish(place, parts, steps):
    subs, columns = len(parts), len(parts[0])
    rows, width = parts[0][0].shape
    return pl.pallas_call(
        functools.partial(finish_kernel, subs, columns),
        grid=(1,),
        in_specs=[pl.BlockSpec(memory_space=pltpu.SMEM)]
        + [pl.BlockSpec((rows, width), lambda i: (0, 0))] * (subs * columns),
        out_specs=pl.BlockSpec((steps, rows // steps, width * subs), lambda i: (0, 0, 0)),
        out_shape=jax.ShapeDtypeStruct((steps, rows // steps, width * subs), BF16),
        compiler_params=params(),
    )(place, *[p for several in parts for p in several])


def swap(x, axis, offset, count):
    return lax.ppermute(x, axis, [(i, i ^ offset) for i in range(count)])


def gather(x, subs):
    return [x] + [swap(x, "sub", k, subs) for k in range(1, subs)]


def gather_middle(x):
    return lax.ppermute(x, "sub", [(1, 2), (2, 1)])


def gather_ends(two):
    return lax.ppermute(two, "sub", [(2, 3), (1, 0)])


def add(a, b):
    return (a.astype(F32) + b.astype(F32)).astype(BF16)


def local(
    tokens, norm_gain, copy_ids, gate_scores, inner_codes, inner_scales, down_codes, down_scales
):
    eps, subs, groups = lax.axis_size("ep"), lax.axis_size("sub"), lax.axis_size("grp")
    slots = inner_codes.shape[0]
    steps, rows, top = copy_ids.shape
    units = inner_codes.shape[3]
    experts = eps * slots
    capacity = (3 * rows * top + 2 * experts - 1) // (2 * experts)
    columns = eps // 2
    place = jnp.stack([lax.axis_index("ep"), lax.axis_index("sub")]).astype(jnp.int32)
    group = steps * rows

    packed = pack(tokens, norm_gain, copy_ids, gate_scores)
    near = [packed] + [swap(packed, "sub", k, subs) for k in range(1, subs)]
    codes = jnp.transpose(inner_codes, (0, 2, 3, 1)).reshape(slots * 2, units, -1)
    scales = jnp.transpose(inner_scales, (0, 2, 3, 1)).reshape(slots * 2, units, -1)
    inner_weights, mark = dequant(codes, scales, packed)
    inner_weights = inner_weights.reshape(slots, 2, units, -1)
    outer_codes = jnp.transpose(down_codes, (0, 2, 1))
    outer_scales = jnp.transpose(down_scales, (0, 2, 1))
    line = columns == 2 and subs == 4
    first_across = [swap(packed, "ep", 2, eps)] if line else []
    own = join(near, [mark] + first_across)[0]
    other = swap(own, "ep", 1, eps)

    capacity_rows = group * subs * 2 // rows * slots * capacity

    def plan(first, count, holds):
        return Plan(first, count, holds, slots, subs, group, top, eps)

    if line and capacity_rows % 384 == 0:
        most = 2 * capacity_rows
        first = capacity_rows // 384 * 256
        second = capacity_rows
        last = most - first - second
        holds = (first,)
        plan0, plan1 = plan(0, first, holds), plan(first, second, holds)
        plan2 = plan(first + second, last, holds)
        pair = [own, other]
        _, rows0, *mixed0 = rows_in(plan0, place, [pair])
        act0, mark = inner(plan0, rows0, mixed0[0], inner_weights, [])
        one0, two0 = swap(act0, "sub", 1, subs), swap(act0, "sub", 2, subs)
        middle0 = gather_middle(act0)
        pieces = first_across + [swap(n, "ep", 2, eps) for n in near[1:]]
        moved = join(pieces, [mark], 4)
        everything = [pair, list(moved) + [swap(m, "ep", 1, eps) for m in moved]]
        longest, *several = rows_in(
            plan(first, second + last, holds), place, everything, (second, last)
        )
        rows1, rows2 = several[0], several[4]
        mixed1, mixed2 = several[1:4], several[5:]
        act1, _ = inner(plan1, rows1, mixed1[0], inner_weights, [])
        act1 = join([act1], [one0, two0, middle0])[0]
        one1, two1 = swap(act1, "sub", 1, subs), swap(act1, "sub", 2, subs)
        parts0 = [act0, one0, two0, middle0, gather_ends(two0)]
        for shift in range(1, groups):
            moved = lax.ppermute(
                longest, "grp", [(i, (i + shift) % groups) for i in range(groups)]
            )
            longest = jnp.maximum(longest, moved)
        outer_weights, _ = dequant(outer_codes, outer_scales, act1, subs)
        sums = outer(plan0, place, mixed0, parts0, [], outer_weights, columns)

        passed = join([act1], [two1, sums[0]])[0]
        parts1 = [gather_middle(passed), gather_ends(two1)]
        first1 = outer_part(plan1, place, mixed1[0], [act1, one1, two1], outer_weights, [passed])

        def more(kept, sent):
            act, _ = inner(plan2, rows2, mixed2[0], inner_weights, [kept])
            return tuple(
                outer(plan2, place, mixed2, gather(act, subs), [kept, sent], outer_weights, columns)
            )

        sums = lax.cond(
            longest[0, 0] > float(first + second), more, lambda a, b: (a, b), *sums
        )
        keep, send = outer(plan1, place, mixed1, parts1, sums, outer_weights, columns, first1)
    else:
        count = -(-capacity_rows // LANES) * LANES
        each = plan(0, count, ())
        outer_weights, _ = dequant(outer_codes, outer_scales, own, subs)
        keeps, sends = [], []
        across = [swap(own, "ep", 2 * j, eps) for j in range(1, columns)]
        held = [[own, other]] + [[a, swap(a, "ep", 1, eps)] for a in across]
        for pair in held:
            _, rows_here, *mixed = rows_in(each, place, [pair])
            act, _ = inner(each, rows_here, mixed[0], inner_weights, [])
            kept, sent = outer(each, place, mixed, gather(act, subs), [], outer_weights, 1)
            keeps.append(kept)
            sends.append(sent)
        keep, send = jnp.concatenate(keeps, axis=0), jnp.concatenate(sends, axis=0)

    chip = add(keep, swap(send, "ep", 1, eps))
    chip = chip.reshape(columns, subs, group, -1)
    arrived = []
    for k in range(subs):
        arrived.append([])
        for j in range(columns):
            pairs = []
            for e in range(eps):
                for z in range(subs):
                    pairs.append((e * subs + z, (e ^ (2 * j)) * subs + (z ^ k)))
            block = chip[j, k]
            arrived[-1].append(lax.ppermute(block, ("ep", "sub"), pairs) if j + k else block)
    return finish(place, arrived, steps)


def solution(mesh):
    return jax.shard_map(
        local,
        mesh=mesh,
        in_specs=(
            P(None, ("grp", "ep", "sub"), None),
            P(),
            P(None, ("grp", "ep", "sub"), None),
            P(None, ("grp", "ep", "sub"), None),
            P("ep", None, None, "sub"),
            P("ep", None, None, "sub"),
            P("ep", None, "sub"),
            P("ep", None, "sub"),
        ),
        out_specs=P(None, ("grp", "ep", "sub"), None),
        check_vma=False,
    )
```

profile of v0, /device:TPU:0, one launch (start us, length us, event | category | flops | bytes accessed | tf_op | source)
XLA Modules:
  0.0 142.5 jit_solution(2120209336224439743)
XLA Ops:
  0.0 1.2 shard_map.82._after_ref.refs_0_
  1.2 3.1 %collective-permute-start.3 = (bf16[32,2944]{1,0:T(8,128)(2,1)S(1)}, bf16[32,2944]{1,0:T(8,128)(2,1)S(1)}, u32[]{:S(2)}, u32[]{:S(2)}) collective-permute-start(bf16[32,2944]{1,0:T(8,128)(2,1)S(1)} %shard_map.82._after_ref.refs_0_), channel_id=1, source_target_pairs={{0,1},{1,0},{2,3},{3,2},{4,5},{5,4},{6,7},{7,6},{8,9},{9,8},{10,11... | collective-permute-start | bytes 565256 | tf_op jit(solution)/shard_map/ppermute | solution.py:541
  4.2 2.6 %collective-permute-start.4 = (bf16[32,2944]{1,0:T(8,128)(2,1)S(1)}, bf16[32,2944]{1,0:T(8,128)(2,1)S(1)}, u32[]{:S(2)}, u32[]{:S(2)}) collective-permute-start(bf16[32,2944]{1,0:T(8,128)(2,1)S(1)} %shard_map.82._after_ref.refs_0_), channel_id=1, source_target_pairs={{0,2},{1,3},{2,0},{3,1},{4,6},{5,7},{6,4},{7,5},{8,10},{9,11},{10,... | collective-permute-start | bytes 565256 | tf_op jit(solution)/shard_map/ppermute | solution.py:541
  6.8 1.7 %collective-permute-start.6 = (bf16[32,2944]{1,0:T(8,128)(2,1)S(1)}, bf16[32,2944]{1,0:T(8,128)(2,1)S(1)}, u32[]{:S(2)}, u32[]{:S(2)}) collective-permute-start(bf16[32,2944]{1,0:T(8,128)(2,1)S(1)} %shard_map.82._after_ref.refs_0_), channel_id=1, source_target_pairs={{0,8},{4,12},{8,0},{12,4},{1,9},{5,13},{9,1},{13,5},{2,10},{6,14},... | collective-permute-start | bytes 565256 | tf_op jit(solution)/shard_map/ppermute | solution.py:541
  8.5 1.5 %copy.9 = bf16[2,2,720,90]{3,2,1,0:T(8,128)(2,1)S(1)} copy(bf16[2,2,720,90]{2,1,3,0:T(2,128)(2,1)} %bitcast.38) | data formatting | bytes 1036800 | tf_op jit(solution)/shard_map/transpose | solution.py:576
  10.1 13.3 %shard_map.83 = (bf16[4,720,2880]{2,1,0:T(8,128)(2,1)}, f32[8,128]{1,0:T(8,128)S(1)}) custom-call(bf16[4,720,2880]{2,1,0:T(8,128)(2,1)} %bitcast.35, bf16[4,720,90]{2,1,0:T(8,128)(2,1)S(1)} %bitcast.30, bf16[32,2944]{1,0:T(8,128)(2,1)S(1)} %shard_map.82._after_ref.refs_0_), custom_call_target="tpu_custom_call" | custom-call | flops 1024 | bytes 1024 | tf_op jit(solution)/shard_map/pallas_call | solution.py:103
  23.9 1.7 %collective-permute-start.8 = (bf16[32,2944]{1,0:T(8,128)(2,1)S(1)}, bf16[32,2944]{1,0:T(8,128)(2,1)S(1)}, u32[]{:S(2)}, u32[]{:S(2)}) collective-permute-start(bf16[32,2944]{1,0:T(8,128)(2,1)S(1)} %collective-permute-done.3.refs_1_), channel_id=1, source_target_pairs={{0,8},{4,12},{8,0},{12,4},{1,9},{5,13},{9,1},{13,5},{2,10},{6,14},... | collective-permute-start | bytes 565256 | tf_op jit(solution)/shard_map/ppermute | solution.py:541
  26.1 2.8 %shard_map.85 = (f32[8,128]{1,0:T(8,128)}, bf16[2880,256]{1,0:T(8,128)(2,1)S(1)}, f32[8,256]{1,0:T(8,128)S(1)}, bf16[256,256]{1,0:T(8,128)(2,1)S(1)}, bf16[256,256]{1,0:T(8,128)(2,1)S(1)}) custom-call(s32[2]{0:T(128)S(1)} %pad_add_fusion.place_ref, bf16[128,2944]{1,0:T(8,128)(2,1)S(1)} %shard_map.84.refs_0_, bf16[128,2944]{1,0:T(8,128)(2,1)S(1)} %collective-permute-done.7.refs_1_), custom_call_target="tpu_custom_call" | custom-call | flops 1024 | bytes 1024 | tf_op jit(solution)/shard_map/pallas_call | solution.py:322
  28.9 9.2 %shard_map.86 = (bf16[720,256]{1,0:T(8,128)(2,1)S(1)}, f32[8,128]{1,0:T(8,128)S(1)}) custom-call(bf16[2880,256]{1,0:T(8,128)(2,1)S(1)} %get-tuple-element.67.rows_ref, f32[8,256]{1,0:T(8,128)S(1)} %get-tuple-element.68.mask_ref, bf16[2,2,720,2880]{3,2,1,0:T(8,128)(2,1)} %bitcast.32), custom_call_target="tpu_custom_call" | custom-call | flops 1024 | bytes 1024 | tf_op jit(solution)/shard_map/pallas_call | solution.py:360
  41.0 1.1 collective-permute-start.15
  42.1 3.0 %collective-permute-start.16 = (bf16[720,256]{1,0:T(8,128)(2,1)S(1)}, bf16[720,256]{1,0:T(8,128)(2,1)S(1)}, u32[]{:S(2)}, u32[]{:S(2)}) collective-permute-start(bf16[720,256]{1,0:T(8,128)(2,1)S(1)} %get-tuple-element.80.refs_0_), channel_id=1, source_target_pairs={{0,2},{1,3},{2,0},{3,1},{4,6},{5,7},{6,4},{7,5},{8,10},{9,11},{10,... | collective-permute-start | bytes 1105928 | tf_op jit(solution)/shard_map/ppermute | solution.py:541
  47.8 5.5 %shard_map.88 = (f32[8,128]{1,0:T(8,128)S(1)}, bf16[2880,384]{1,0:T(8,128)(2,1)S(1)}, f32[8,384]{1,0:T(8,128)S(1)}, bf16[512,384]{1,0:T(8,128)(2,1)S(1)}, bf16[5...) custom-call(s32[2]{0:T(128)S(1)} %pad_add_fusion.place_ref, ...), custom_call_target="tpu_custom_call" | custom-call | flops 1024 | bytes 1024 | tf_op jit(solution)/shard_map/pallas_call | solution.py:322
  53.4 11.3 %shard_map.89 = (bf16[720,384]{1,0:T(8,128)(2,1)S(1)}, f32[8,128]{1,0:T(8,128)}) custom-call(bf16[2880,384]{1,0:T(8,128)(2,1)S(1)} %get-tuple-element.78.rows_ref, f32[8,384]{1,0:T(8,128)S(1)} %get-tuple-element.75.mask_ref, bf16[2,2,720,2880]{3,2,1,0:T(8,128)(2,1)S(1)} %bitcast.34), custom_call_target="tpu_custom_call" | custom-call | flops 1024 | bytes 1024 | tf_op jit(solution)/shard_map/pallas_call | solution.py:360
  64.8 6.4 %collective-permute-start.18 = (bf16[720,384]{1,0:T(8,128)(2,1)S(1)}, bf16[720,384]{1,0:T(8,128)(2,1)S(1)}, u32[]{:S(2)}, u32[]{:S(2)}) collective-permute-start(bf16[720,384]{1,0:T(8,128)(2,1)S(1)} %shard_map.90._after_ref.refs_0_), channel_id=1, source_target_pairs={{0,2},{1,3},{2,0},{3,1},{4,6},{5,7},{6,4},{7,5},{8,10},{9,11},{10,... | collective-permute-start | bytes 1658888 | tf_op jit(solution)/shard_map/ppermute | solution.py:541
  71.2 1.5 %collective-permute-start.19 = (bf16[720,256]{1,0:T(8,128)(2,1)S(1)}, bf16[720,256]{1,0:T(8,128)(2,1)}, u32[]{:S(2)}, u32[]{:S(2)}) collective-permute-start(bf16[720,256]{1,0:T(8,128)(2,1)S(1)} %collective-permute-done.16.refs_2_), channel_id=1, source_target_pairs={{2,3},{1,0},{6,7},{5,4},{10,11},{9,8},{14,15},{13,12},{18,19},{17,... | collective-permute-start | bytes 1105928 | tf_op jit(solution)/shard_map/ppermute | solution.py:553
  72.7 1.6 %collective-permute-start.23 = (f32[8,128]{1,0:T(8,128)S(1)}, f32[8,128]{1,0:T(8,128)S(1)}, u32[]{:S(2)}, u32[]{:S(2)}) collective-permute-start(f32[8,128]{1,0:T(8,128)S(1)} %get-tuple-element.85), channel_id=1, source_target_pairs={{0,16},{16,0},{1,17},{17,1},{2,18},{18,2},{3,19},{19,3},{4,20},{20... | collective-permute-start | bytes 12296 | tf_op jit(solution)/shard_map/ppermute | solution.py:617
  74.6 1.8 %collective-permute-done.23 = f32[8,128]{1,0:T(8,128)S(1)} collective-permute-done((f32[8,128]{1,0:T(8,128)S(1)}, f32[8,128]{1,0:T(8,128)S(1)}, u32[]{:S(2)}, u32[]{:S(2)}) %collective-permute-start.23) | collective-permute-done | bytes 4128 | tf_op jit(solution)/shard_map/ppermute | solution.py:617
  77.5 3.2 %collective-permute-start.22 = (bf16[720,384]{1,0:T(8,128)(2,1)S(1)}, bf16[720,384]{1,0:T(8,128)(2,1)S(1)}, u32[]{:S(2)}, u32[]{:S(2)}) collective-permute-start(bf16[720,384]{1,0:T(8,128)(2,1)S(1)} %shard_map.90._after_ref.refs_0_), channel_id=1, source_target_pairs={{0,1},{1,0},{2,3},{3,2},{4,5},{5,4},{6,7},{7,6},{8,9},{9,8},{10,11... | collective-permute-start | bytes 1658888 | tf_op jit(solution)/shard_map/ppermute | solution.py:541
  80.7 11.0 %shard_map.91 = (bf16[2,4,720,720]{3,2,1,0:T(8,128)(2,1)}, f32[8,128]{1,0:T(8,128)}) custom-call(bf16[2,720,2880]{2,1,0:T(8,128)(2,1)} %bitcast.36, bf16[2,720,90]{2,1,0:T(8,128)(2,1)S(1)} %bitcast.31, bf16[720,384]{1,0:T(8,128)(2,1)S(1)} %shard_map.90._after_ref.refs_0_), custom_call_target="tpu_custom_call" | custom-call | flops 1024 | bytes 1024 | tf_op jit(solution)/shard_map/pallas_call | solution.py:103
  91.7 3.6 %collective-permute-done.19.refs_4_ = bf16[720,256]{1,0:T(8,128)(2,1)} collective-permute-done((bf16[720,256]{1,0:T(8,128)(2,1)S(1)}, bf16[720,256]{1,0:T(8,128)(2,1)}, u32[]{:S(2)}, u32[]{:S(2)}) %collective-permute-start.19) | collective-permute-done | bytes 368672 | tf_op jit(solution)/shard_map/ppermute | solution.py:553
  95.2 9.0 %shard_map.92 = (bf16[2,128,720]{2,1,0:T(8,128)(2,1)}, bf16[2,128,720]{2,1,0:T(8,128)(2,1)}) custom-call(s32[2]{0:T(128)S(1)} %copy-done.9, f32[8,256]{1,0:T(8,128)S(1)} %get-tuple-element.68.mask_ref, bf16[256,256]{1,0:T(8,128)(2,1)} %copy-done.4, bf16[256,256]{1,0:T(8,128)(2,1)} %copy-done.5, bf16[720,256]{1,0:T(8,128)(2,1)S(1)} %get-tuple-element.80.refs_0_, ...), custom_call_target="tpu_custom_call" | custom-call | flops 1024 | bytes 1024 | tf_op jit(solution)/shard_map/pallas_call | solution.py:462
  106.0 1.3 collective-permute-start.21
  107.3 8.0 %shard_map.94.refs_2_ = f32[720,384]{1,0:T(8,128)S(1)} custom-call(s32[2]{0:T(128)S(1)} %copy-done.10, f32[8,384]{1,0:T(8,128)S(1)} %get-tuple-element.75.mask_ref, bf16[720,384]{1,0:T(8,128)(2,1)S(1)} %shard_map.90._after_ref.refs_0_, bf16[720,384]{1,0:T(8,128)(2,1)S(1)} %collective-permute-done.22.refs_1_, ...), custom_call_target="tpu_custom_call" | custom-call | flops 1024 | bytes 1024 | tf_op jit(solution)/shard_map/pallas_call | solution.py:462
  115.4 2.0 %collective-permute-done.21.refs_1_ = bf16[720,384]{1,0:T(8,128)(2,1)S(1)} collective-permute-done((bf16[720,384]{1,0:T(8,128)(2,1)S(1)}, bf16[720,384]{1,0:T(8,128)(2,1)S(1)}, u32[]{:S(2)}, u32[]{:S(2)}) %collective-permute-start.21) | collective-permute-done | bytes 552992 | tf_op jit(solution)/shard_map/ppermute | solution.py:553
  117.4 7.2 %shard_map.95 = (bf16[2,128,720]{2,1,0:T(8,128)(2,1)S(1)}, bf16[2,128,720]{2,1,0:T(8,128)(2,1)S(1)}) custom-call(s32[2]{0:T(128)S(1)} %copy-done.10, f32[8,384]{1,0:T(8,128)S(1)} %get-tuple-element.75.mask_ref, bf16[512,384]{1,0:T(8,128)(2,1)} %copy-done, bf16[512,384]{1,0:T(8,128)(2,1)} %copy-done.1, bf16[720,384]{1,0:T(8,128)(2,1)S(1)} %collective-permute-done.20.refs_0_, ...), custom_call_target="tpu_custom_call" | custom-call | flops 1024 | bytes 1024 | tf_op jit(solution)/shard_map/pallas_call | solution.py:462
  124.6 1.7 %collective-permute-done.24 = bf16[2,128,720]{2,1,0:T(8,128)(2,1)S(1)} collective-permute-done((bf16[2,128,720]{2,1,0:T(8,128)(2,1)S(1)}, bf16[2,128,720]{2,1,0:T(8,128)(2,1)S(1)}, u32[]{:S(2)}, u32[]{:S(2)}) %collective-permute-start.24) | collective-permute-done | bytes 368672 | tf_op jit(solution)/shard_map/ppermute | solution.py:541
  128.3 1.7 %collective-permute-start.27 = (bf16[32,720]{1,0:T(8,128)(2,1)S(1)}, bf16[32,720]{1,0:T(8,128)(2,1)S(1)}, u32[]{:S(2)}, u32[]{:S(2)}) collective-permute-start(bf16[32,720]{1,0:T(8,128)(2,1)S(1)} %get-tuple-element.99), channel_id=1, source_target_pairs={{0,9},{1,8},{2,11},{3,10},{4,13},{5,12},{6,15},{7,14},{8,1},{9,0},... | collective-permute-start | bytes 138248 | tf_op jit(solution)/shard_map/ppermute | solution.py:664
  130.1 3.4 %collective-permute-start.29 = (bf16[32,720]{1,0:T(8,128)(2,1)S(1)}, bf16[32,720]{1,0:T(8,128)(2,1)S(1)}, u32[]{:S(2)}, u32[]{:S(2)}) collective-permute-start(bf16[32,720]{1,0:T(8,128)(2,1)S(1)} %get-tuple-element.97), channel_id=1, source_target_pairs={{0,10},{1,11},{2,8},{3,9},{4,14},{5,15},{6,12},{7,13},{8,2},{9,3},... | collective-permute-start | bytes 138248 | tf_op jit(solution)/shard_map/ppermute | solution.py:664
  134.2 3.5 %collective-permute-start.31 = (bf16[32,720]{1,0:T(8,128)(2,1)S(1)}, bf16[32,720]{1,0:T(8,128)(2,1)S(1)}, u32[]{:S(2)}, u32[]{:S(2)}) collective-permute-start(bf16[32,720]{1,0:T(8,128)(2,1)S(1)} %get-tuple-element.95), channel_id=1, source_target_pairs={{0,11},{1,10},{2,9},{3,8},{4,15},{5,14},{6,13},{7,12},{8,3},{9,2},... | collective-permute-start | bytes 138248 | tf_op jit(solution)/shard_map/ppermute | solution.py:664
  137.7 1.6 %collective-permute-done.29.refs_5_ = bf16[32,720]{1,0:T(8,128)(2,1)S(1)} collective-permute-done((bf16[32,720]{1,0:T(8,128)(2,1)S(1)}, bf16[32,720]{1,0:T(8,128)(2,1)S(1)}, u32[]{:S(2)}, u32[]{:S(2)}) %collective-permute-start.29) | collective-permute-done | bytes 46112 | tf_op jit(solution)/shard_map/ppermute | solution.py:664
  139.5 1.7 %collective-permute-done.31.refs_7_ = bf16[32,720]{1,0:T(8,128)(2,1)S(1)} collective-permute-done((bf16[32,720]{1,0:T(8,128)(2,1)S(1)}, bf16[32,720]{1,0:T(8,128)(2,1)S(1)}, u32[]{:S(2)}, u32[]{:S(2)}) %collective-permute-start.31) | collective-permute-done | bytes 46112 | tf_op jit(solution)/shard_map/ppermute | solution.py:664
  141.1 1.4 shard_map.96
  (72 shorter events, 13.1 us)
Async XLA Ops:
  1.2 22.2 %collective-permute-start.3 = (bf16[32,2944]{1,0:T(8,128)(2,1)S(1)}, bf16[32,2944]{1,0:T(8,128)(2,1)S(1)}, u32[]{:S(2)}, u32[]{:S(2)}) collective-permute-start(bf16[32,2944]{1,0:T(8,128)(2,1)S(1)} %shard_map.82._after_ref.refs_0_), channel_id=1, source_target_pairs={{0,1},{1,0},{2,3},{3,2},{4,5},{5,4},{6,7},{7,6},{8,9},{9,8},{10,11... | collective-permute-start | bytes 565256 | tf_op jit(solution)/shard_map/ppermute | solution.py:541
  4.2 19.2 %collective-permute-start.4 = (bf16[32,2944]{1,0:T(8,128)(2,1)S(1)}, bf16[32,2944]{1,0:T(8,128)(2,1)S(1)}, u32[]{:S(2)}, u32[]{:S(2)}) collective-permute-start(bf16[32,2944]{1,0:T(8,128)(2,1)S(1)} %shard_map.82._after_ref.refs_0_), channel_id=1, source_target_pairs={{0,2},{1,3},{2,0},{3,1},{4,6},{5,7},{6,4},{7,5},{8,10},{9,11},{10,... | collective-permute-start | bytes 565256 | tf_op jit(solution)/shard_map/ppermute | solution.py:541
  6.8 16.6 %collective-permute-start.5 = (bf16[32,2944]{1,0:T(8,128)(2,1)S(1)}, bf16[32,2944]{1,0:T(8,128)(2,1)S(1)}, u32[]{:S(2)}, u32[]{:S(2)}) collective-permute-start(bf16[32,2944]{1,0:T(8,128)(2,1)S(1)} %shard_map.82._after_ref.refs_0_), channel_id=1, source_target_pairs={{0,3},{1,2},{2,1},{3,0},{4,7},{5,6},{6,5},{7,4},{8,11},{9,10},{10,... | collective-permute-start | bytes 565256 | tf_op jit(solution)/shard_map/ppermute | solution.py:541
  6.8 16.6 %collective-permute-start.6 = (bf16[32,2944]{1,0:T(8,128)(2,1)S(1)}, bf16[32,2944]{1,0:T(8,128)(2,1)S(1)}, u32[]{:S(2)}, u32[]{:S(2)}) collective-permute-start(bf16[32,2944]{1,0:T(8,128)(2,1)S(1)} %shard_map.82._after_ref.refs_0_), channel_id=1, source_target_pairs={{0,8},{4,12},{8,0},{12,4},{1,9},{5,13},{9,1},{13,5},{2,10},{6,14},... | collective-permute-start | bytes 565256 | tf_op jit(solution)/shard_map/ppermute | solution.py:541
  23.5 2.6 %collective-permute-start.7 = (bf16[128,2944]{1,0:T(8,128)(2,1)S(1)}, bf16[128,2944]{1,0:T(8,128)(2,1)S(1)}, u32[]{:S(2)}, u32[]{:S(2)}) collective-permute-start(bf16[128,2944]{1,0:T(8,128)(2,1)S(1)} %shard_map.84.refs_0_), channel_id=1, source_target_pairs={{0,4},{4,0},{8,12},{12,8},{1,5},{5,1},{9,13},{13,9},{2,6},{6,2},{1... | collective-permute-start | bytes 2261000 | tf_op jit(solution)/shard_map/ppermute | solution.py:541
  23.6 14.5 %collective-permute-start.10 = (bf16[32,2944]{1,0:T(8,128)(2,1)S(1)}, bf16[32,2944]{1,0:T(8,128)(2,1)S(1)}, u32[]{:S(2)}, u32[]{:S(2)}) collective-permute-start(bf16[32,2944]{1,0:T(8,128)(2,1)S(1)} %collective-permute-done.5.refs_3_), channel_id=1, source_target_pairs={{0,8},{4,12},{8,0},{12,4},{1,9},{5,13},{9,1},{13,5},{2,10},{6,14},... | collective-permute-start | bytes 565256 | tf_op jit(solution)/shard_map/ppermute | solution.py:541
  23.9 14.1 %collective-permute-start.8 = (bf16[32,2944]{1,0:T(8,128)(2,1)S(1)}, bf16[32,2944]{1,0:T(8,128)(2,1)S(1)}, u32[]{:S(2)}, u32[]{:S(2)}) collective-permute-start(bf16[32,2944]{1,0:T(8,128)(2,1)S(1)} %collective-permute-done.3.refs_1_), channel_id=1, source_target_pairs={{0,8},{4,12},{8,0},{12,4},{1,9},{5,13},{9,1},{13,5},{2,10},{6,14},... | collective-permute-start | bytes 565256 | tf_op jit(solution)/shard_map/ppermute | solution.py:541
  25.7 13.1 %collective-permute-start.9 = (bf16[32,2944]{1,0:T(8,128)(2,1)S(1)}, bf16[32,2944]{1,0:T(8,128)(2,1)S(1)}, u32[]{:S(2)}, u32[]{:S(2)}) collective-permute-start(bf16[32,2944]{1,0:T(8,128)(2,1)S(1)} %collective-permute-done.4.refs_2_), channel_id=1, source_target_pairs={{0,8},{4,12},{8,0},{12,4},{1,9},{5,13},{9,1},{13,5},{2,10},{6,14},... | collective-permute-start | bytes 565256 | tf_op jit(solution)/shard_map/ppermute | solution.py:541
  26.1 21.8 %copy-start.8 = (s32[2]{0:T(128)}, s32[2]{0:T(128)S(1)}, u32[]{:S(2)}) copy-start(s32[2]{0:T(128)S(1)} %pad_add_fusion.place_ref) | copy-start | bytes 28
  28.9 24.5 %copy-start.6 = (bf16[4,720,2880]{2,1,0:T(8,128)(2,1)S(1)}, bf16[4,720,2880]{2,1,0:T(8,128)(2,1)}, u32[]{:S(2)}) copy-start(bf16[4,720,2880]{2,1,0:T(8,128)(2,1)} %get-tuple-element.69) | copy-start | bytes 49766404
  40.4 5.6 %collective-permute-start.11 = (bf16[32,2944]{1,0:T(8,128)(2,1)S(1)}, bf16[32,2944]{1,0:T(8,128)(2,1)S(1)}, u32[]{:S(2)}, u32[]{:S(2)}) collective-permute-start(bf16[32,2944]{1,0:T(8,128)(2,1)S(1)} %get-tuple-element.71.refs_2_), channel_id=1, source_target_pairs={{0,4},{4,0},{8,12},{12,8},{1,5},{5,1},{9,13},{13,9},{2,6},{6,2},{1... | collective-permute-start | bytes 565256 | tf_op jit(solution)/shard_map/ppermute | solution.py:541
  40.5 5.6 %collective-permute-start.12 = (bf16[32,2944]{1,0:T(8,128)(2,1)S(1)}, bf16[32,2944]{1,0:T(8,128)(2,1)S(1)}, u32[]{:S(2)}, u32[]{:S(2)}) collective-permute-start(bf16[32,2944]{1,0:T(8,128)(2,1)S(1)} %get-tuple-element.72.refs_3_), channel_id=1, source_target_pairs={{0,4},{4,0},{8,12},{12,8},{1,5},{5,1},{9,13},{13,9},{2,6},{6,2},{1... | collective-permute-start | bytes 565256 | tf_op jit(solution)/shard_map/ppermute | solution.py:541
  41.0 23.7 %collective-permute-start.15 = (bf16[720,256]{1,0:T(8,128)(2,1)S(1)}, bf16[720,256]{1,0:T(8,128)(2,1)S(1)}, u32[]{:S(2)}, u32[]{:S(2)}) collective-permute-start(bf16[720,256]{1,0:T(8,128)(2,1)S(1)} %get-tuple-element.80.refs_0_), channel_id=1, source_target_pairs={{0,1},{1,0},{2,3},{3,2},{4,5},{5,4},{6,7},{7,6},{8,9},{9,8},{10,11... | collective-permute-start | bytes 1105928 | tf_op jit(solution)/shard_map/ppermute | solution.py:541
  42.1 22.6 %collective-permute-start.16 = (bf16[720,256]{1,0:T(8,128)(2,1)S(1)}, bf16[720,256]{1,0:T(8,128)(2,1)S(1)}, u32[]{:S(2)}, u32[]{:S(2)}) collective-permute-start(bf16[720,256]{1,0:T(8,128)(2,1)S(1)} %get-tuple-element.80.refs_0_), channel_id=1, source_target_pairs={{0,2},{1,3},{2,0},{3,1},{4,6},{5,7},{6,4},{7,5},{8,10},{9,11},{10,... | collective-permute-start | bytes 1105928 | tf_op jit(solution)/shard_map/ppermute | solution.py:541
  45.2 19.5 %collective-permute-start.17 = (bf16[720,256]{1,0:T(8,128)(2,1)S(1)}, bf16[720,256]{1,0:T(8,128)(2,1)S(1)}, u32[]{:S(2)}, u32[]{:S(2)}) collective-permute-start(bf16[720,256]{1,0:T(8,128)(2,1)S(1)} %get-tuple-element.80.refs_0_), channel_id=1, source_target_pairs={{1,2},{2,1},{5,6},{6,5},{9,10},{10,9},{13,14},{14,13},{17,18},{18,... | collective-permute-start | bytes 1105928 | tf_op jit(solution)/shard_map/ppermute | solution.py:549
  46.1 1.5 %collective-permute-start.13 = (bf16[32,2944]{1,0:T(8,128)(2,1)S(1)}, bf16[32,2944]{1,0:T(8,128)(2,1)S(1)}, u32[]{:S(2)}, u32[]{:S(2)}) collective-permute-start(bf16[32,2944]{1,0:T(8,128)(2,1)S(1)} %get-tuple-element.73.refs_4_), channel_id=1, source_target_pairs={{0,4},{4,0},{8,12},{12,8},{1,5},{5,1},{9,13},{13,9},{2,6},{6,2},{1... | collective-permute-start | bytes 565256 | tf_op jit(solution)/shard_map/ppermute | solution.py:541
  46.1 1.7 %collective-permute-start.14 = (bf16[32,2944]{1,0:T(8,128)(2,1)S(1)}, bf16[32,2944]{1,0:T(8,128)(2,1)S(1)}, u32[]{:S(2)}, u32[]{:S(2)}) collective-permute-start(bf16[32,2944]{1,0:T(8,128)(2,1)S(1)} %get-tuple-element.74.refs_5_), channel_id=1, source_target_pairs={{0,4},{4,0},{8,12},{12,8},{1,5},{5,1},{9,13},{13,9},{2,6},{6,2},{1... | collective-permute-start | bytes 565256 | tf_op jit(solution)/shard_map/ppermute | solution.py:541
  64.7 30.6 %copy-start.9 = (s32[2]{0:T(128)S(1)}, s32[2]{0:T(128)}, u32[]{:S(2)}) copy-start(s32[2]{0:T(128)} %copy-done.8) | copy-start | bytes 28
  64.8 40.4 %collective-permute-start.18 = (bf16[720,384]{1,0:T(8,128)(2,1)S(1)}, bf16[720,384]{1,0:T(8,128)(2,1)S(1)}, u32[]{:S(2)}, u32[]{:S(2)}) collective-permute-start(bf16[720,384]{1,0:T(8,128)(2,1)S(1)} %shard_map.90._after_ref.refs_0_), channel_id=1, source_target_pairs={{0,2},{1,3},{2,0},{3,1},{4,6},{5,7},{6,4},{7,5},{8,10},{9,11},{10,... | collective-permute-start | bytes 1658888 | tf_op jit(solution)/shard_map/ppermute | solution.py:541
  71.2 24.1 %collective-permute-start.19 = (bf16[720,256]{1,0:T(8,128)(2,1)S(1)}, bf16[720,256]{1,0:T(8,128)(2,1)}, u32[]{:S(2)}, u32[]{:S(2)}) collective-permute-start(bf16[720,256]{1,0:T(8,128)(2,1)S(1)} %collective-permute-done.16.refs_2_), channel_id=1, source_target_pairs={{2,3},{1,0},{6,7},{5,4},{10,11},{9,8},{14,15},{13,12},{18,19},{17,... | collective-permute-start | bytes 1105928 | tf_op jit(solution)/shard_map/ppermute | solution.py:553
  72.7 3.7 %collective-permute-start.23 = (f32[8,128]{1,0:T(8,128)S(1)}, f32[8,128]{1,0:T(8,128)S(1)}, u32[]{:S(2)}, u32[]{:S(2)}) collective-permute-start(f32[8,128]{1,0:T(8,128)S(1)} %get-tuple-element.85), channel_id=1, source_target_pairs={{0,16},{16,0},{1,17},{17,1},{2,18},{18,2},{3,19},{19,3},{4,20},{20... | collective-permute-start | bytes 12296 | tf_op jit(solution)/shard_map/ppermute | solution.py:617
  77.5 29.8 %collective-permute-start.22 = (bf16[720,384]{1,0:T(8,128)(2,1)S(1)}, bf16[720,384]{1,0:T(8,128)(2,1)S(1)}, u32[]{:S(2)}, u32[]{:S(2)}) collective-permute-start(bf16[720,384]{1,0:T(8,128)(2,1)S(1)} %shard_map.90._after_ref.refs_0_), channel_id=1, source_target_pairs={{0,1},{1,0},{2,3},{3,2},{4,5},{5,4},{6,7},{7,6},{8,9},{9,8},{10,11... | collective-permute-start | bytes 1658888 | tf_op jit(solution)/shard_map/ppermute | solution.py:541
  105.3 10.1 %collective-permute-start.20 = (bf16[720,384]{1,0:T(8,128)(2,1)S(1)}, bf16[720,384]{1,0:T(8,128)(2,1)S(1)}, u32[]{:S(2)}, u32[]{:S(2)}) collective-permute-start(bf16[720,384]{1,0:T(8,128)(2,1)S(1)} %shard_map.93.refs_4_), channel_id=1, source_target_pairs={{1,2},{2,1},{5,6},{6,5},{9,10},{10,9},{13,14},{14,13},{17,18},{18,... | collective-permute-start | bytes 1658888 | tf_op jit(solution)/shard_map/ppermute | solution.py:549
  106.0 11.4 %collective-permute-start.21 = (bf16[720,384]{1,0:T(8,128)(2,1)S(1)}, bf16[720,384]{1,0:T(8,128)(2,1)S(1)}, u32[]{:S(2)}, u32[]{:S(2)}) collective-permute-start(bf16[720,384]{1,0:T(8,128)(2,1)S(1)} %collective-permute-done.18.refs_1_.refs_2_), channel_id=1, source_target_pairs={{2,3},{1,0},{6,7},{5,4},{10,11},{9,8},{14,15},{13,12},{18,19},{17,... | collective-permute-start | bytes 1658888 | tf_op jit(solution)/shard_map/ppermute | solution.py:553
  124.6 1.8 %collective-permute-start.24 = (bf16[2,128,720]{2,1,0:T(8,128)(2,1)S(1)}, bf16[2,128,720]{2,1,0:T(8,128)(2,1)S(1)}, u32[]{:S(2)}, u32[]{:S(2)}) collective-permute-start(bf16[2,128,720]{2,1,0:T(8,128)(2,1)S(1)} %get-tuple-element.94), channel_id=1, source_target_pairs={{0,4},{4,0},{8,12},{12,8},{1,5},{5,1},{9,13},{13,9},{2,6},{6,2},{1... | collective-permute-start | bytes 1105928 | tf_op jit(solution)/shard_map/ppermute | solution.py:541
  126.5 7.0 %collective-permute-start.25 = (bf16[32,720]{1,0:T(8,128)(2,1)S(1)}, bf16[32,720]{1,0:T(8,128)(2,1)S(1)}, u32[]{:S(2)}, u32[]{:S(2)}) collective-permute-start(bf16[32,720]{1,0:T(8,128)(2,1)S(1)} %get-tuple-element.101), channel_id=1, source_target_pairs={{0,8},{1,9},{2,10},{3,11},{4,12},{5,13},{6,14},{7,15},{8,0},{9,1},... | collective-permute-start | bytes 138248 | tf_op jit(solution)/shard_map/ppermute | solution.py:664
  127.6 6.6 %collective-permute-start.26 = (bf16[32,720]{1,0:T(8,128)(2,1)S(1)}, bf16[32,720]{1,0:T(8,128)(2,1)S(1)}, u32[]{:S(2)}, u32[]{:S(2)}) collective-permute-start(bf16[32,720]{1,0:T(8,128)(2,1)S(1)} %get-tuple-element.100), channel_id=1, source_target_pairs={{0,1},{1,0},{2,3},{3,2},{4,5},{5,4},{6,7},{7,6},{8,9},{9,8},{10,11... | collective-permute-start | bytes 138248 | tf_op jit(solution)/shard_map/ppermute | solution.py:664
  128.3 9.4 %collective-permute-start.27 = (bf16[32,720]{1,0:T(8,128)(2,1)S(1)}, bf16[32,720]{1,0:T(8,128)(2,1)S(1)}, u32[]{:S(2)}, u32[]{:S(2)}) collective-permute-start(bf16[32,720]{1,0:T(8,128)(2,1)S(1)} %get-tuple-element.99), channel_id=1, source_target_pairs={{0,9},{1,8},{2,11},{3,10},{4,13},{5,12},{6,15},{7,14},{8,1},{9,0},... | collective-permute-start | bytes 138248 | tf_op jit(solution)/shard_map/ppermute | solution.py:664
  130.1 7.7 %collective-permute-start.28 = (bf16[32,720]{1,0:T(8,128)(2,1)S(1)}, bf16[32,720]{1,0:T(8,128)(2,1)S(1)}, u32[]{:S(2)}, u32[]{:S(2)}) collective-permute-start(bf16[32,720]{1,0:T(8,128)(2,1)S(1)} %get-tuple-element.98), channel_id=1, source_target_pairs={{0,2},{1,3},{2,0},{3,1},{4,6},{5,7},{6,4},{7,5},{8,10},{9,11},{10,... | collective-permute-start | bytes 138248 | tf_op jit(solution)/shard_map/ppermute | solution.py:664
  130.1 9.2 %collective-permute-start.29 = (bf16[32,720]{1,0:T(8,128)(2,1)S(1)}, bf16[32,720]{1,0:T(8,128)(2,1)S(1)}, u32[]{:S(2)}, u32[]{:S(2)}) collective-permute-start(bf16[32,720]{1,0:T(8,128)(2,1)S(1)} %get-tuple-element.97), channel_id=1, source_target_pairs={{0,10},{1,11},{2,8},{3,9},{4,14},{5,15},{6,12},{7,13},{8,2},{9,3},... | collective-permute-start | bytes 138248 | tf_op jit(solution)/shard_map/ppermute | solution.py:664
  133.5 6.0 %collective-permute-start.30 = (bf16[32,720]{1,0:T(8,128)(2,1)S(1)}, bf16[32,720]{1,0:T(8,128)(2,1)S(1)}, u32[]{:S(2)}, u32[]{:S(2)}) collective-permute-start(bf16[32,720]{1,0:T(8,128)(2,1)S(1)} %get-tuple-element.96), channel_id=1, source_target_pairs={{0,3},{1,2},{2,1},{3,0},{4,7},{5,6},{6,5},{7,4},{8,11},{9,10},{10,... | collective-permute-start | bytes 138248 | tf_op jit(solution)/shard_map/ppermute | solution.py:664
  134.2 6.9 %collective-permute-start.31 = (bf16[32,720]{1,0:T(8,128)(2,1)S(1)}, bf16[32,720]{1,0:T(8,128)(2,1)S(1)}, u32[]{:S(2)}, u32[]{:S(2)}) collective-permute-start(bf16[32,720]{1,0:T(8,128)(2,1)S(1)} %get-tuple-element.95), channel_id=1, source_target_pairs={{0,11},{1,10},{2,9},{3,8},{4,15},{5,14},{6,13},{7,12},{8,3},{9,2},... | collective-permute-start | bytes 138248 | tf_op jit(solution)/shard_map/ppermute | solution.py:664
  (8 other events, 66.5 us)
where the time goes:
time: 143 us
  Pallas kernels  80 us (56%)
  starting transfers between devices  41.9 us (29%)
  waiting for transfers between devices  14.4 us (10%)
  local copies, waits for them, and re-layouts  5.04 us (4%)
    ppermute x17, starting transfers between devices, swap(): return lax.ppermute(x, axis, [(i, i ^ offset) for i in range(count)])  24.8 us
    pallas_call x2, Pallas kernels, dequant(): pl.pallas_call(dequant_kernel, grid=(count,), in_specs=[pl.BlockSpec((1,...  24.3 us
    pallas_call x3, Pallas kernels, outer_call(): pl.pallas_call(kernel, grid_spec=pltpu.PrefetchScalarGridSpec(num_scalar_...  24.2 us
    pallas_call x2, Pallas kernels, inner(): pl.pallas_call(functools.partial(inner_kernel, plan), grid=(units // bloc...  20.4 us
    ppermute x7, starting transfers between devices, local(): lax.ppermute(block, ('ep', 'sub'), pairs)  11.2 us
    pallas_call x2, Pallas kernels, rows_in(): pl.pallas_call(functools.partial(rows_kernel, plan, layout), grid=(1,), i...  8.37 us
    ppermute x2, waiting for transfers between devices, gather_ends(): return lax.ppermute(two, 'sub', [(2, 3), (1, 0)])  5.57 us
    ppermute x17, waiting for transfers between devices, swap(): return lax.ppermute(x, axis, [(i, i ^ offset) for i in range(count)])  3.61 us
  transfers between devices with their start and end apart: 29, of which 10 were waited for; matrix products, arithmetic and copies ran while one was open for 2% of the time, Pallas kernels for 49%

commit v1 on v0

--- a/solution.py
+++ b/solution.py
@@ -473,7 +473,7 @@
         out_shape=shapes,
         compiler_params=params(),
         cost_estimate=HINT,
-    )(place, *operands, in_hbm(weights), *after)
+    )(place, *operands, weights, *after)
 
 
 def outer_part(plan, place, mask, parts, weights, after):

time: 143 us -> 141 us (0.986)
  Pallas kernels: 80 us -> 75.1 us
  waiting for transfers between devices: 14.4 us -> 16.9 us
    pallas_call x3, Pallas kernels: 24.2 us -> 21.3 us  [outer_call(): pl.pallas_call(kernel, grid_spec=pltpu.PrefetchScalarGridSpec(num_scalar_...]
    pallas_call x2, Pallas kernels: 24.3 us -> 22.2 us  [dequant(): pl.pallas_call(dequant_kernel, grid=(count,), in_specs=[pl.BlockSpec((1,...]
    ppermute x2, waiting for transfers between devices: 5.57 us -> 7.39 us  [gather_ends(): return lax.ppermute(two, 'sub', [(2, 3), (1, 0)])]
  transfers between devices with their start and end apart: 29 -> 29, of which waited for: 10 -> 11; matrix products, arithmetic and copies ran while one was open for 2% -> 2% of each run, Pallas kernels for 49% -> 47%
where the time goes in v1:
time: 141 us; the launch traced here: 140 us
  Pallas kernels  75.1 us (53%)
  starting transfers between devices  42.2 us (30%)
  waiting for transfers between devices  16.9 us (12%)
  local copies, waits for them, and re-layouts  5.06 us (4%)
    ppermute x17, starting transfers between devices, swap(): return lax.ppermute(x, axis, [(i, i ^ offset) for i in range(count)])  24.7 us
    pallas_call x2, Pallas kernels, dequant(): pl.pallas_call(dequant_kernel, grid=(count,), in_specs=[pl.BlockSpec((1,...  22.2 us
    pallas_call x3, Pallas kernels, outer_call(): pl.pallas_call(kernel, grid_spec=pltpu.PrefetchScalarGridSpec(num_scalar_...  21.3 us
    pallas_call x2, Pallas kernels, inner(): pl.pallas_call(functools.partial(inner_kernel, plan), grid=(units // bloc...  20.4 us
    ppermute x7, starting transfers between devices, local(): lax.ppermute(block, ('ep', 'sub'), pairs)  11.2 us
    pallas_call x2, Pallas kernels, rows_in(): pl.pallas_call(functools.partial(rows_kernel, plan, layout), grid=(1,), i...  8.4 us
    ppermute x2, waiting for transfers between devices, gather_ends(): return lax.ppermute(two, 'sub', [(2, 3), (1, 0)])  7.39 us
    ppermute x17, waiting for transfers between devices, swap(): return lax.ppermute(x, axis, [(i, i ^ offset) for i in range(count)])  4.49 us
  transfers between devices with their start and end apart: 29, of which 11 were waited for; matrix products, arithmetic and copies ran while one was open for 2% of the time, Pallas kernels for 47%

profile of v1, /device:TPU:0, one launch (start us, length us, event | category | flops | bytes accessed | tf_op | source)
XLA Modules:
  0.0 140.5 jit_solution(15667327674770786411)
XLA Ops:
  0.0 1.2 shard_map.82._after_ref.refs_0_
  1.2 3.1 %collective-permute-start.3 = (bf16[32,2944]{1,0:T(8,128)(2,1)S(1)}, bf16[32,2944]{1,0:T(8,128)(2,1)S(1)}, u32[]{:S(2)}, u32[]{:S(2)}) collective-permute-start(bf16[32,2944]{1,0:T(8,128)(2,1)S(1)} %shard_map.82._after_ref.refs_0_), channel_id=1, source_target_pairs={{0,1},{1,0},{2,3},{3,2},{4,5},{5,4},{6,7},{7,6},{8,9},{9,8},{10,11... | collective-permute-start | bytes 565256 | tf_op jit(solution)/shard_map/ppermute | solution.py:541
  4.2 2.6 %collective-permute-start.4 = (bf16[32,2944]{1,0:T(8,128)(2,1)S(1)}, bf16[32,2944]{1,0:T(8,128)(2,1)S(1)}, u32[]{:S(2)}, u32[]{:S(2)}) collective-permute-start(bf16[32,2944]{1,0:T(8,128)(2,1)S(1)} %shard_map.82._after_ref.refs_0_), channel_id=1, source_target_pairs={{0,2},{1,3},{2,0},{3,1},{4,6},{5,7},{6,4},{7,5},{8,10},{9,11},{10,... | collective-permute-start | bytes 565256 | tf_op jit(solution)/shard_map/ppermute | solution.py:541
  6.8 1.7 %collective-permute-start.6 = (bf16[32,2944]{1,0:T(8,128)(2,1)S(1)}, bf16[32,2944]{1,0:T(8,128)(2,1)S(1)}, u32[]{:S(2)}, u32[]{:S(2)}) collective-permute-start(bf16[32,2944]{1,0:T(8,128)(2,1)S(1)} %shard_map.82._after_ref.refs_0_), channel_id=1, source_target_pairs={{0,8},{4,12},{8,0},{12,4},{1,9},{5,13},{9,1},{13,5},{2,10},{6,14},... | collective-permute-start | bytes 565256 | tf_op jit(solution)/shard_map/ppermute | solution.py:541
  8.5 1.5 %copy.9 = bf16[2,2,720,90]{3,2,1,0:T(8,128)(2,1)S(1)} copy(bf16[2,2,720,90]{2,1,3,0:T(2,128)(2,1)} %bitcast.38) | data formatting | bytes 1036800 | tf_op jit(solution)/shard_map/transpose | solution.py:576
  10.1 13.3 %shard_map.83 = (bf16[4,720,2880]{2,1,0:T(8,128)(2,1)}, f32[8,128]{1,0:T(8,128)S(1)}) custom-call(bf16[4,720,2880]{2,1,0:T(8,128)(2,1)} %bitcast.35, bf16[4,720,90]{2,1,0:T(8,128)(2,1)S(1)} %bitcast.30, bf16[32,2944]{1,0:T(8,128)(2,1)S(1)} %shard_map.82._after_ref.refs_0_), custom_call_target="tpu_custom_call" | custom-call | flops 1024 | bytes 1024 | tf_op jit(solution)/shard_map/pallas_call | solution.py:103
  24.0 1.7 %collective-permute-start.8 = (bf16[32,2944]{1,0:T(8,128)(2,1)S(1)}, bf16[32,2944]{1,0:T(8,128)(2,1)S(1)}, u32[]{:S(2)}, u32[]{:S(2)}) collective-permute-start(bf16[32,2944]{1,0:T(8,128)(2,1)S(1)} %collective-permute-done.3.refs_1_), channel_id=1, source_target_pairs={{0,8},{4,12},{8,0},{12,4},{1,9},{5,13},{9,1},{13,5},{2,10},{6,14},... | collective-permute-start | bytes 565256 | tf_op jit(solution)/shard_map/ppermute | solution.py:541
  26.1 2.8 %shard_map.85 = (f32[8,128]{1,0:T(8,128)}, bf16[2880,256]{1,0:T(8,128)(2,1)S(1)}, f32[8,256]{1,0:T(8,128)S(1)}, bf16[256,256]{1,0:T(8,128)(2,1)S(1)}, bf16[256,256]{1,0:T(8,128)(2,1)S(1)}) custom-call(s32[2]{0:T(128)S(1)} %pad_add_fusion.place_ref, bf16[128,2944]{1,0:T(8,128)(2,1)S(1)} %shard_map.84.refs_0_, bf16[128,2944]{1,0:T(8,128)(2,1)S(1)} %collective-permute-done.7.refs_1_), custom_call_target="tpu_custom_call" | custom-call | flops 1024 | bytes 1024 | tf_op jit(solution)/shard_map/pallas_call | solution.py:322
  28.9 9.2 %shard_map.86 = (bf16[720,256]{1,0:T(8,128)(2,1)S(1)}, f32[8,128]{1,0:T(8,128)S(1)}) custom-call(bf16[2880,256]{1,0:T(8,128)(2,1)S(1)} %get-tuple-element.67.rows_ref, f32[8,256]{1,0:T(8,128)S(1)} %get-tuple-element.68.mask_ref, bf16[2,2,720,2880]{3,2,1,0:T(8,128)(2,1)} %bitcast.32), custom_call_target="tpu_custom_call" | custom-call | flops 1024 | bytes 1024 | tf_op jit(solution)/shard_map/pallas_call | solution.py:360
  42.1 3.0 %collective-permute-start.16 = (bf16[720,256]{1,0:T(8,128)(2,1)S(1)}, bf16[720,256]{1,0:T(8,128)(2,1)S(1)}, u32[]{:S(2)}, u32[]{:S(2)}) collective-permute-start(bf16[720,256]{1,0:T(8,128)(2,1)S(1)} %get-tuple-element.80.refs_0_), channel_id=1, source_target_pairs={{0,2},{1,3},{2,0},{3,1},{4,6},{5,7},{6,4},{7,5},{8,10},{9,11},{10,... | collective-permute-start | bytes 1105928 | tf_op jit(solution)/shard_map/ppermute | solution.py:541
  47.8 5.6 %shard_map.88 = (f32[8,128]{1,0:T(8,128)S(1)}, bf16[2880,384]{1,0:T(8,128)(2,1)S(1)}, f32[8,384]{1,0:T(8,128)S(1)}, bf16[512,384]{1,0:T(8,128)(2,1)S(1)}, bf16[5...) custom-call(s32[2]{0:T(128)S(1)} %pad_add_fusion.place_ref, ...), custom_call_target="tpu_custom_call" | custom-call | flops 1024 | bytes 1024 | tf_op jit(solution)/shard_map/pallas_call | solution.py:322
  53.4 11.3 %shard_map.89 = (bf16[720,384]{1,0:T(8,128)(2,1)S(1)}, f32[8,128]{1,0:T(8,128)}) custom-call(bf16[2880,384]{1,0:T(8,128)(2,1)S(1)} %get-tuple-element.78.rows_ref, f32[8,384]{1,0:T(8,128)S(1)} %get-tuple-element.75.mask_ref, bf16[2,2,720,2880]{3,2,1,0:T(8,128)(2,1)S(1)} %bitcast.34), custom_call_target="tpu_custom_call" | custom-call | flops 1024 | bytes 1024 | tf_op jit(solution)/shard_map/pallas_call | solution.py:360
  64.8 6.3 %collective-permute-start.18 = (bf16[720,384]{1,0:T(8,128)(2,1)S(1)}, bf16[720,384]{1,0:T(8,128)(2,1)S(1)}, u32[]{:S(2)}, u32[]{:S(2)}) collective-permute-start(bf16[720,384]{1,0:T(8,128)(2,1)S(1)} %shard_map.90._after_ref.refs_0_), channel_id=1, source_target_pairs={{0,2},{1,3},{2,0},{3,1},{4,6},{5,7},{6,4},{7,5},{8,10},{9,11},{10,... | collective-permute-start | bytes 1658888 | tf_op jit(solution)/shard_map/ppermute | solution.py:541
  71.2 1.5 %collective-permute-start.19 = (bf16[720,256]{1,0:T(8,128)(2,1)S(1)}, bf16[720,256]{1,0:T(8,128)(2,1)}, u32[]{:S(2)}, u32[]{:S(2)}) collective-permute-start(bf16[720,256]{1,0:T(8,128)(2,1)S(1)} %collective-permute-done.16.refs_2_), channel_id=1, source_target_pairs={{2,3},{1,0},{6,7},{5,4},{10,11},{9,8},{14,15},{13,12},{18,19},{17,... | collective-permute-start | bytes 1105928 | tf_op jit(solution)/shard_map/ppermute | solution.py:553
  72.7 1.6 %collective-permute-start.23 = (f32[8,128]{1,0:T(8,128)S(1)}, f32[8,128]{1,0:T(8,128)S(1)}, u32[]{:S(2)}, u32[]{:S(2)}) collective-permute-start(f32[8,128]{1,0:T(8,128)S(1)} %get-tuple-element.85), channel_id=1, source_target_pairs={{0,16},{16,0},{1,17},{17,1},{2,18},{18,2},{3,19},{19,3},{4,20},{20... | collective-permute-start | bytes 12296 | tf_op jit(solution)/shard_map/ppermute | solution.py:617
  74.6 1.8 %collective-permute-done.23 = f32[8,128]{1,0:T(8,128)S(1)} collective-permute-done((f32[8,128]{1,0:T(8,128)S(1)}, f32[8,128]{1,0:T(8,128)S(1)}, u32[]{:S(2)}, u32[]{:S(2)}) %collective-permute-start.23) | collective-permute-done | bytes 4128 | tf_op jit(solution)/shard_map/ppermute | solution.py:617
  77.5 3.2 %collective-permute-start.22 = (bf16[720,384]{1,0:T(8,128)(2,1)S(1)}, bf16[720,384]{1,0:T(8,128)(2,1)S(1)}, u32[]{:S(2)}, u32[]{:S(2)}) collective-permute-start(bf16[720,384]{1,0:T(8,128)(2,1)S(1)} %shard_map.90._after_ref.refs_0_), channel_id=1, source_target_pairs={{0,1},{1,0},{2,3},{3,2},{4,5},{5,4},{6,7},{7,6},{8,9},{9,8},{10,11... | collective-permute-start | bytes 1658888 | tf_op jit(solution)/shard_map/ppermute | solution.py:541
  80.7 8.9 %shard_map.91 = (bf16[2,4,720,720]{3,2,1,0:T(8,128)(2,1)S(1)}, f32[8,128]{1,0:T(8,128)}) custom-call(bf16[2,720,2880]{2,1,0:T(8,128)(2,1)} %bitcast.36, bf16[2,720,90]{2,1,0:T(8,128)(2,1)S(1)} %bitcast.31, bf16[720,384]{1,0:T(8,128)(2,1)S(1)} %shard_map.90._after_ref.refs_0_), custom_call_target="tpu_custom_call" | custom-call | flops 1024 | bytes 1024 | tf_op jit(solution)/shard_map/pallas_call | solution.py:103
  89.6 5.7 %collective-permute-done.19.refs_4_ = bf16[720,256]{1,0:T(8,128)(2,1)} collective-permute-done((bf16[720,256]{1,0:T(8,128)(2,1)S(1)}, bf16[720,256]{1,0:T(8,128)(2,1)}, u32[]{:S(2)}, u32[]{:S(2)}) %collective-permute-start.19) | collective-permute-done | bytes 368672 | tf_op jit(solution)/shard_map/ppermute | solution.py:553
  95.3 7.4 %shard_map.92 = (bf16[2,128,720]{2,1,0:T(8,128)(2,1)}, bf16[2,128,720]{2,1,0:T(8,128)(2,1)}) custom-call(s32[2]{0:T(128)S(1)} %copy-done.11, f32[8,256]{1,0:T(8,128)S(1)} %get-tuple-element.68.mask_ref, bf16[256,256]{1,0:T(8,128)(2,1)} %copy-done.4, bf16[256,256]{1,0:T(8,128)(2,1)} %copy-done.5, bf16[720,256]{1,0:T(8,128)(2,1)S(1)} %get-tuple-element.80.refs_0_, ...), custom_call_target="tpu_custom_call" | custom-call | flops 1024 | bytes 1024 | tf_op jit(solution)/shard_map/pallas_call | solution.py:462
  104.5 1.6 %collective-permute-start.21 = (bf16[720,384]{1,0:T(8,128)(2,1)S(1)}, bf16[720,384]{1,0:T(8,128)(2,1)S(1)}, u32[]{:S(2)}, u32[]{:S(2)}) collective-permute-start(bf16[720,384]{1,0:T(8,128)(2,1)S(1)} %collective-permute-done.18.refs_1_.refs_2_), channel_id=1, source_target_pairs={{2,3},{1,0},{6,7},{5,4},{10,11},{9,8},{14,15},{13,12},{18,19},{17,... | collective-permute-start | bytes 1658888 | tf_op jit(solution)/shard_map/ppermute | solution.py:553
  107.0 8.0 %shard_map.94.refs_2_ = f32[720,384]{1,0:T(8,128)S(1)} custom-call(s32[2]{0:T(128)S(1)} %copy-done.12, f32[8,384]{1,0:T(8,128)S(1)} %get-tuple-element.75.mask_ref, bf16[720,384]{1,0:T(8,128)(2,1)S(1)} %shard_map.90._after_ref.refs_0_, bf16[720,384]{1,0:T(8,128)(2,1)S(1)} %collective-permute-done.22.refs_1_, ...), custom_call_target="tpu_custom_call" | custom-call | flops 1024 | bytes 1024 | tf_op jit(solution)/shard_map/pallas_call | solution.py:462
  115.1 1.7 %collective-permute-done.21.refs_1_ = bf16[720,384]{1,0:T(8,128)(2,1)S(1)} collective-permute-done((bf16[720,384]{1,0:T(8,128)(2,1)S(1)}, bf16[720,384]{1,0:T(8,128)(2,1)S(1)}, u32[]{:S(2)}, u32[]{:S(2)}) %collective-permute-start.21) | collective-permute-done | bytes 552992 | tf_op jit(solution)/shard_map/ppermute | solution.py:553
  116.8 5.9 %shard_map.95 = (bf16[2,128,720]{2,1,0:T(8,128)(2,1)S(1)}, bf16[2,128,720]{2,1,0:T(8,128)(2,1)S(1)}) custom-call(s32[2]{0:T(128)S(1)} %copy-done.12, f32[8,384]{1,0:T(8,128)S(1)} %get-tuple-element.75.mask_ref, bf16[512,384]{1,0:T(8,128)(2,1)} %copy-done, bf16[512,384]{1,0:T(8,128)(2,1)} %copy-done.1, bf16[720,384]{1,0:T(8,128)(2,1)S(1)} %collective-permute-done.20.refs_0_, ...), custom_call_target="tpu_custom_call" | custom-call | flops 1024 | bytes 1024 | tf_op jit(solution)/shard_map/pallas_call | solution.py:462
  122.8 1.7 %collective-permute-done.24 = bf16[2,128,720]{2,1,0:T(8,128)(2,1)S(1)} collective-permute-done((bf16[2,128,720]{2,1,0:T(8,128)(2,1)S(1)}, bf16[2,128,720]{2,1,0:T(8,128)(2,1)S(1)}, u32[]{:S(2)}, u32[]{:S(2)}) %collective-permute-start.24) | collective-permute-done | bytes 368672 | tf_op jit(solution)/shard_map/ppermute | solution.py:541
  124.6 1.1 collective-permute-start.25
  125.9 2.3 %collective-permute-start.27 = (bf16[32,720]{1,0:T(8,128)(2,1)S(1)}, bf16[32,720]{1,0:T(8,128)(2,1)S(1)}, u32[]{:S(2)}, u32[]{:S(2)}) collective-permute-start(bf16[32,720]{1,0:T(8,128)(2,1)S(1)} %get-tuple-element.99), channel_id=1, source_target_pairs={{0,9},{1,8},{2,11},{3,10},{4,13},{5,12},{6,15},{7,14},{8,1},{9,0},... | collective-permute-start | bytes 138248 | tf_op jit(solution)/shard_map/ppermute | solution.py:664
  128.2 3.4 %collective-permute-start.29 = (bf16[32,720]{1,0:T(8,128)(2,1)S(1)}, bf16[32,720]{1,0:T(8,128)(2,1)S(1)}, u32[]{:S(2)}, u32[]{:S(2)}) collective-permute-start(bf16[32,720]{1,0:T(8,128)(2,1)S(1)} %get-tuple-element.97), channel_id=1, source_target_pairs={{0,10},{1,11},{2,8},{3,9},{4,14},{5,15},{6,12},{7,13},{8,2},{9,3},... | collective-permute-start | bytes 138248 | tf_op jit(solution)/shard_map/ppermute | solution.py:664
  132.2 3.6 %collective-permute-start.31 = (bf16[32,720]{1,0:T(8,128)(2,1)S(1)}, bf16[32,720]{1,0:T(8,128)(2,1)S(1)}, u32[]{:S(2)}, u32[]{:S(2)}) collective-permute-start(bf16[32,720]{1,0:T(8,128)(2,1)S(1)} %get-tuple-element.95), channel_id=1, source_target_pairs={{0,11},{1,10},{2,9},{3,8},{4,15},{5,14},{6,13},{7,12},{8,3},{9,2},... | collective-permute-start | bytes 138248 | tf_op jit(solution)/shard_map/ppermute | solution.py:664
  135.8 1.1 collective-permute-done.29.refs_5_
  137.6 1.5 %collective-permute-done.31.refs_7_ = bf16[32,720]{1,0:T(8,128)(2,1)S(1)} collective-permute-done((bf16[32,720]{1,0:T(8,128)(2,1)S(1)}, bf16[32,720]{1,0:T(8,128)(2,1)S(1)}, u32[]{:S(2)}, u32[]{:S(2)}) %collective-permute-start.31) | collective-permute-done | bytes 46112 | tf_op jit(solution)/shard_map/ppermute | solution.py:664
  139.1 1.4 shard_map.96
  (76 shorter events, 13.8 us)
Async XLA Ops:
  1.2 22.2 %collective-permute-start.3 = (bf16[32,2944]{1,0:T(8,128)(2,1)S(1)}, bf16[32,2944]{1,0:T(8,128)(2,1)S(1)}, u32[]{:S(2)}, u32[]{:S(2)}) collective-permute-start(bf16[32,2944]{1,0:T(8,128)(2,1)S(1)} %shard_map.82._after_ref.refs_0_), channel_id=1, source_target_pairs={{0,1},{1,0},{2,3},{3,2},{4,5},{5,4},{6,7},{7,6},{8,9},{9,8},{10,11... | collective-permute-start | bytes 565256 | tf_op jit(solution)/shard_map/ppermute | solution.py:541
  4.2 19.2 %collective-permute-start.4 = (bf16[32,2944]{1,0:T(8,128)(2,1)S(1)}, bf16[32,2944]{1,0:T(8,128)(2,1)S(1)}, u32[]{:S(2)}, u32[]{:S(2)}) collective-permute-start(bf16[32,2944]{1,0:T(8,128)(2,1)S(1)} %shard_map.82._after_ref.refs_0_), channel_id=1, source_target_pairs={{0,2},{1,3},{2,0},{3,1},{4,6},{5,7},{6,4},{7,5},{8,10},{9,11},{10,... | collective-permute-start | bytes 565256 | tf_op jit(solution)/shard_map/ppermute | solution.py:541
  6.8 16.6 %collective-permute-start.5 = (bf16[32,2944]{1,0:T(8,128)(2,1)S(1)}, bf16[32,2944]{1,0:T(8,128)(2,1)S(1)}, u32[]{:S(2)}, u32[]{:S(2)}) collective-permute-start(bf16[32,2944]{1,0:T(8,128)(2,1)S(1)} %shard_map.82._after_ref.refs_0_), channel_id=1, source_target_pairs={{0,3},{1,2},{2,1},{3,0},{4,7},{5,6},{6,5},{7,4},{8,11},{9,10},{10,... | collective-permute-start | bytes 565256 | tf_op jit(solution)/shard_map/ppermute | solution.py:541
  6.8 16.6 %collective-permute-start.6 = (bf16[32,2944]{1,0:T(8,128)(2,1)S(1)}, bf16[32,2944]{1,0:T(8,128)(2,1)S(1)}, u32[]{:S(2)}, u32[]{:S(2)}) collective-permute-start(bf16[32,2944]{1,0:T(8,128)(2,1)S(1)} %shard_map.82._after_ref.refs_0_), channel_id=1, source_target_pairs={{0,8},{4,12},{8,0},{12,4},{1,9},{5,13},{9,1},{13,5},{2,10},{6,14},... | collective-permute-start | bytes 565256 | tf_op jit(solution)/shard_map/ppermute | solution.py:541
  23.5 2.6 %collective-permute-start.7 = (bf16[128,2944]{1,0:T(8,128)(2,1)S(1)}, bf16[128,2944]{1,0:T(8,128)(2,1)S(1)}, u32[]{:S(2)}, u32[]{:S(2)}) collective-permute-start(bf16[128,2944]{1,0:T(8,128)(2,1)S(1)} %shard_map.84.refs_0_), channel_id=1, source_target_pairs={{0,4},{4,0},{8,12},{12,8},{1,5},{5,1},{9,13},{13,9},{2,6},{6,2},{1... | collective-permute-start | bytes 2261000 | tf_op jit(solution)/shard_map/ppermute | solution.py:541
  23.6 14.5 %collective-permute-start.10 = (bf16[32,2944]{1,0:T(8,128)(2,1)S(1)}, bf16[32,2944]{1,0:T(8,128)(2,1)S(1)}, u32[]{:S(2)}, u32[]{:S(2)}) collective-permute-start(bf16[32,2944]{1,0:T(8,128)(2,1)S(1)} %collective-permute-done.5.refs_3_), channel_id=1, source_target_pairs={{0,8},{4,12},{8,0},{12,4},{1,9},{5,13},{9,1},{13,5},{2,10},{6,14},... | collective-permute-start | bytes 565256 | tf_op jit(solution)/shard_map/ppermute | solution.py:541
  24.0 14.1 %collective-permute-start.8 = (bf16[32,2944]{1,0:T(8,128)(2,1)S(1)}, bf16[32,2944]{1,0:T(8,128)(2,1)S(1)}, u32[]{:S(2)}, u32[]{:S(2)}) collective-permute-start(bf16[32,2944]{1,0:T(8,128)(2,1)S(1)} %collective-permute-done.3.refs_1_), channel_id=1, source_target_pairs={{0,8},{4,12},{8,0},{12,4},{1,9},{5,13},{9,1},{13,5},{2,10},{6,14},... | collective-permute-start | bytes 565256 | tf_op jit(solution)/shard_map/ppermute | solution.py:541
  25.7 13.1 %collective-permute-start.9 = (bf16[32,2944]{1,0:T(8,128)(2,1)S(1)}, bf16[32,2944]{1,0:T(8,128)(2,1)S(1)}, u32[]{:S(2)}, u32[]{:S(2)}) collective-permute-start(bf16[32,2944]{1,0:T(8,128)(2,1)S(1)} %collective-permute-done.4.refs_2_), channel_id=1, source_target_pairs={{0,8},{4,12},{8,0},{12,4},{1,9},{5,13},{9,1},{13,5},{2,10},{6,14},... | collective-permute-start | bytes 565256 | tf_op jit(solution)/shard_map/ppermute | solution.py:541
  26.1 21.8 %copy-start.10 = (s32[2]{0:T(128)}, s32[2]{0:T(128)S(1)}, u32[]{:S(2)}) copy-start(s32[2]{0:T(128)S(1)} %pad_add_fusion.place_ref) | copy-start | bytes 28
  28.9 24.5 %copy-start.6 = (bf16[4,720,2880]{2,1,0:T(8,128)(2,1)S(1)}, bf16[4,720,2880]{2,1,0:T(8,128)(2,1)}, u32[]{:S(2)}) copy-start(bf16[4,720,2880]{2,1,0:T(8,128)(2,1)} %get-tuple-element.69) | copy-start | bytes 49766404
  40.4 5.6 %collective-permute-start.11 = (bf16[32,2944]{1,0:T(8,128)(2,1)S(1)}, bf16[32,2944]{1,0:T(8,128)(2,1)S(1)}, u32[]{:S(2)}, u32[]{:S(2)}) collective-permute-start(bf16[32,2944]{1,0:T(8,128)(2,1)S(1)} %get-tuple-element.71.refs_2_), channel_id=1, source_target_pairs={{0,4},{4,0},{8,12},{12,8},{1,5},{5,1},{9,13},{13,9},{2,6},{6,2},{1... | collective-permute-start | bytes 565256 | tf_op jit(solution)/shard_map/ppermute | solution.py:541
  40.5 5.6 %collective-permute-start.12 = (bf16[32,2944]{1,0:T(8,128)(2,1)S(1)}, bf16[32,2944]{1,0:T(8,128)(2,1)S(1)}, u32[]{:S(2)}, u32[]{:S(2)}) collective-permute-start(bf16[32,2944]{1,0:T(8,128)(2,1)S(1)} %get-tuple-element.72.refs_3_), channel_id=1, source_target_pairs={{0,4},{4,0},{8,12},{12,8},{1,5},{5,1},{9,13},{13,9},{2,6},{6,2},{1... | collective-permute-start | bytes 565256 | tf_op jit(solution)/shard_map/ppermute | solution.py:541
  41.0 23.7 %collective-permute-start.15 = (bf16[720,256]{1,0:T(8,128)(2,1)S(1)}, bf16[720,256]{1,0:T(8,128)(2,1)S(1)}, u32[]{:S(2)}, u32[]{:S(2)}) collective-permute-start(bf16[720,256]{1,0:T(8,128)(2,1)S(1)} %get-tuple-element.80.refs_0_), channel_id=1, source_target_pairs={{0,1},{1,0},{2,3},{3,2},{4,5},{5,4},{6,7},{7,6},{8,9},{9,8},{10,11... | collective-permute-start | bytes 1105928 | tf_op jit(solution)/shard_map/ppermute | solution.py:541
  42.1 22.6 %collective-permute-start.16 = (bf16[720,256]{1,0:T(8,128)(2,1)S(1)}, bf16[720,256]{1,0:T(8,128)(2,1)S(1)}, u32[]{:S(2)}, u32[]{:S(2)}) collective-permute-start(bf16[720,256]{1,0:T(8,128)(2,1)S(1)} %get-tuple-element.80.refs_0_), channel_id=1, source_target_pairs={{0,2},{1,3},{2,0},{3,1},{4,6},{5,7},{6,4},{7,5},{8,10},{9,11},{10,... | collective-permute-start | bytes 1105928 | tf_op jit(solution)/shard_map/ppermute | solution.py:541
  45.2 19.6 %collective-permute-start.17 = (bf16[720,256]{1,0:T(8,128)(2,1)S(1)}, bf16[720,256]{1,0:T(8,128)(2,1)S(1)}, u32[]{:S(2)}, u32[]{:S(2)}) collective-permute-start(bf16[720,256]{1,0:T(8,128)(2,1)S(1)} %get-tuple-element.80.refs_0_), channel_id=1, source_target_pairs={{1,2},{2,1},{5,6},{6,5},{9,10},{10,9},{13,14},{14,13},{17,18},{18,... | collective-permute-start | bytes 1105928 | tf_op jit(solution)/shard_map/ppermute | solution.py:549
  46.1 1.5 %collective-permute-start.13 = (bf16[32,2944]{1,0:T(8,128)(2,1)S(1)}, bf16[32,2944]{1,0:T(8,128)(2,1)S(1)}, u32[]{:S(2)}, u32[]{:S(2)}) collective-permute-start(bf16[32,2944]{1,0:T(8,128)(2,1)S(1)} %get-tuple-element.73.refs_4_), channel_id=1, source_target_pairs={{0,4},{4,0},{8,12},{12,8},{1,5},{5,1},{9,13},{13,9},{2,6},{6,2},{1... | collective-permute-start | bytes 565256 | tf_op jit(solution)/shard_map/ppermute | solution.py:541
  46.2 1.7 %collective-permute-start.14 = (bf16[32,2944]{1,0:T(8,128)(2,1)S(1)}, bf16[32,2944]{1,0:T(8,128)(2,1)S(1)}, u32[]{:S(2)}, u32[]{:S(2)}) collective-permute-start(bf16[32,2944]{1,0:T(8,128)(2,1)S(1)} %get-tuple-element.74.refs_5_), channel_id=1, source_target_pairs={{0,4},{4,0},{8,12},{12,8},{1,5},{5,1},{9,13},{13,9},{2,6},{6,2},{1... | collective-permute-start | bytes 565256 | tf_op jit(solution)/shard_map/ppermute | solution.py:541
  64.7 30.5 %copy-start.11 = (s32[2]{0:T(128)S(1)}, s32[2]{0:T(128)}, u32[]{:S(2)}) copy-start(s32[2]{0:T(128)} %copy-done.10) | copy-start | bytes 28
  64.8 38.8 %collective-permute-start.18 = (bf16[720,384]{1,0:T(8,128)(2,1)S(1)}, bf16[720,384]{1,0:T(8,128)(2,1)S(1)}, u32[]{:S(2)}, u32[]{:S(2)}) collective-permute-start(bf16[720,384]{1,0:T(8,128)(2,1)S(1)} %shard_map.90._after_ref.refs_0_), channel_id=1, source_target_pairs={{0,2},{1,3},{2,0},{3,1},{4,6},{5,7},{6,4},{7,5},{8,10},{9,11},{10,... | collective-permute-start | bytes 1658888 | tf_op jit(solution)/shard_map/ppermute | solution.py:541
  71.2 24.1 %collective-permute-start.19 = (bf16[720,256]{1,0:T(8,128)(2,1)S(1)}, bf16[720,256]{1,0:T(8,128)(2,1)}, u32[]{:S(2)}, u32[]{:S(2)}) collective-permute-start(bf16[720,256]{1,0:T(8,128)(2,1)S(1)} %collective-permute-done.16.refs_2_), channel_id=1, source_target_pairs={{2,3},{1,0},{6,7},{5,4},{10,11},{9,8},{14,15},{13,12},{18,19},{17,... | collective-permute-start | bytes 1105928 | tf_op jit(solution)/shard_map/ppermute | solution.py:553
  72.7 3.7 %collective-permute-start.23 = (f32[8,128]{1,0:T(8,128)S(1)}, f32[8,128]{1,0:T(8,128)S(1)}, u32[]{:S(2)}, u32[]{:S(2)}) collective-permute-start(f32[8,128]{1,0:T(8,128)S(1)} %get-tuple-element.85), channel_id=1, source_target_pairs={{0,16},{16,0},{1,17},{17,1},{2,18},{18,2},{3,19},{19,3},{4,20},{20... | collective-permute-start | bytes 12296 | tf_op jit(solution)/shard_map/ppermute | solution.py:617
  77.5 29.5 %collective-permute-start.22 = (bf16[720,384]{1,0:T(8,128)(2,1)S(1)}, bf16[720,384]{1,0:T(8,128)(2,1)S(1)}, u32[]{:S(2)}, u32[]{:S(2)}) collective-permute-start(bf16[720,384]{1,0:T(8,128)(2,1)S(1)} %shard_map.90._after_ref.refs_0_), channel_id=1, source_target_pairs={{0,1},{1,0},{2,3},{3,2},{4,5},{5,4},{6,7},{7,6},{8,9},{9,8},{10,11... | collective-permute-start | bytes 1658888 | tf_op jit(solution)/shard_map/ppermute | solution.py:541
  103.7 11.3 %collective-permute-start.20 = (bf16[720,384]{1,0:T(8,128)(2,1)S(1)}, bf16[720,384]{1,0:T(8,128)(2,1)S(1)}, u32[]{:S(2)}, u32[]{:S(2)}) collective-permute-start(bf16[720,384]{1,0:T(8,128)(2,1)S(1)} %shard_map.93.refs_4_), channel_id=1, source_target_pairs={{1,2},{2,1},{5,6},{6,5},{9,10},{10,9},{13,14},{14,13},{17,18},{18,... | collective-permute-start | bytes 1658888 | tf_op jit(solution)/shard_map/ppermute | solution.py:549
  104.5 12.2 %collective-permute-start.21 = (bf16[720,384]{1,0:T(8,128)(2,1)S(1)}, bf16[720,384]{1,0:T(8,128)(2,1)S(1)}, u32[]{:S(2)}, u32[]{:S(2)}) collective-permute-start(bf16[720,384]{1,0:T(8,128)(2,1)S(1)} %collective-permute-done.18.refs_1_.refs_2_), channel_id=1, source_target_pairs={{2,3},{1,0},{6,7},{5,4},{10,11},{9,8},{14,15},{13,12},{18,19},{17,... | collective-permute-start | bytes 1658888 | tf_op jit(solution)/shard_map/ppermute | solution.py:553
  122.7 1.8 %collective-permute-start.24 = (bf16[2,128,720]{2,1,0:T(8,128)(2,1)S(1)}, bf16[2,128,720]{2,1,0:T(8,128)(2,1)S(1)}, u32[]{:S(2)}, u32[]{:S(2)}) collective-permute-start(bf16[2,128,720]{2,1,0:T(8,128)(2,1)S(1)} %get-tuple-element.94), channel_id=1, source_target_pairs={{0,4},{4,0},{8,12},{12,8},{1,5},{5,1},{9,13},{13,9},{2,6},{6,2},{1... | collective-permute-start | bytes 1105928 | tf_op jit(solution)/shard_map/ppermute | solution.py:541
  124.6 7.0 %collective-permute-start.25 = (bf16[32,720]{1,0:T(8,128)(2,1)S(1)}, bf16[32,720]{1,0:T(8,128)(2,1)S(1)}, u32[]{:S(2)}, u32[]{:S(2)}) collective-permute-start(bf16[32,720]{1,0:T(8,128)(2,1)S(1)} %get-tuple-element.101), channel_id=1, source_target_pairs={{0,8},{1,9},{2,10},{3,11},{4,12},{5,13},{6,14},{7,15},{8,0},{9,1},... | collective-permute-start | bytes 138248 | tf_op jit(solution)/shard_map/ppermute | solution.py:664
  125.7 6.4 %collective-permute-start.26 = (bf16[32,720]{1,0:T(8,128)(2,1)S(1)}, bf16[32,720]{1,0:T(8,128)(2,1)S(1)}, u32[]{:S(2)}, u32[]{:S(2)}) collective-permute-start(bf16[32,720]{1,0:T(8,128)(2,1)S(1)} %get-tuple-element.100), channel_id=1, source_target_pairs={{0,1},{1,0},{2,3},{3,2},{4,5},{5,4},{6,7},{7,6},{8,9},{9,8},{10,11... | collective-permute-start | bytes 138248 | tf_op jit(solution)/shard_map/ppermute | solution.py:664
  125.9 10.0 %collective-permute-start.27 = (bf16[32,720]{1,0:T(8,128)(2,1)S(1)}, bf16[32,720]{1,0:T(8,128)(2,1)S(1)}, u32[]{:S(2)}, u32[]{:S(2)}) collective-permute-start(bf16[32,720]{1,0:T(8,128)(2,1)S(1)} %get-tuple-element.99), channel_id=1, source_target_pairs={{0,9},{1,8},{2,11},{3,10},{4,13},{5,12},{6,15},{7,14},{8,1},{9,0},... | collective-permute-start | bytes 138248 | tf_op jit(solution)/shard_map/ppermute | solution.py:664
  128.2 7.7 %collective-permute-start.28 = (bf16[32,720]{1,0:T(8,128)(2,1)S(1)}, bf16[32,720]{1,0:T(8,128)(2,1)S(1)}, u32[]{:S(2)}, u32[]{:S(2)}) collective-permute-start(bf16[32,720]{1,0:T(8,128)(2,1)S(1)} %get-tuple-element.98), channel_id=1, source_target_pairs={{0,2},{1,3},{2,0},{3,1},{4,6},{5,7},{6,4},{7,5},{8,10},{9,11},{10,... | collective-permute-start | bytes 138248 | tf_op jit(solution)/shard_map/ppermute | solution.py:664
  128.2 8.8 %collective-permute-start.29 = (bf16[32,720]{1,0:T(8,128)(2,1)S(1)}, bf16[32,720]{1,0:T(8,128)(2,1)S(1)}, u32[]{:S(2)}, u32[]{:S(2)}) collective-permute-start(bf16[32,720]{1,0:T(8,128)(2,1)S(1)} %get-tuple-element.97), channel_id=1, source_target_pairs={{0,10},{1,11},{2,8},{3,9},{4,14},{5,15},{6,12},{7,13},{8,2},{9,3},... | collective-permute-start | bytes 138248 | tf_op jit(solution)/shard_map/ppermute | solution.py:664
  131.6 6.0 %collective-permute-start.30 = (bf16[32,720]{1,0:T(8,128)(2,1)S(1)}, bf16[32,720]{1,0:T(8,128)(2,1)S(1)}, u32[]{:S(2)}, u32[]{:S(2)}) collective-permute-start(bf16[32,720]{1,0:T(8,128)(2,1)S(1)} %get-tuple-element.96), channel_id=1, source_target_pairs={{0,3},{1,2},{2,1},{3,0},{4,7},{5,6},{6,5},{7,4},{8,11},{9,10},{10,... | collective-permute-start | bytes 138248 | tf_op jit(solution)/shard_map/ppermute | solution.py:664
  132.2 6.9 %collective-permute-start.31 = (bf16[32,720]{1,0:T(8,128)(2,1)S(1)}, bf16[32,720]{1,0:T(8,128)(2,1)S(1)}, u32[]{:S(2)}, u32[]{:S(2)}) collective-permute-start(bf16[32,720]{1,0:T(8,128)(2,1)S(1)} %get-tuple-element.95), channel_id=1, source_target_pairs={{0,11},{1,10},{2,9},{3,8},{4,15},{5,14},{6,13},{7,12},{8,3},{9,2},... | collective-permute-start | bytes 138248 | tf_op jit(solution)/shard_map/ppermute | solution.py:664
  (10 other events, 94.0 us)
